TPU v7x, 128 devices: a whole 4x4x4 slice. The times are simulated.
128 devices in a mesh: lon: 16 (over y, z), day: 8 (over x, core).
Axes of the slice: x: 4, y: 4, z: 4, core: 2. Of those that a mesh axis runs over, the one named last changes fastest.
Arguments:
- latent: float32 [32, 1024, 2048], P('day', None, 'lon'), may hold values from -4 to 4
- range_sq: float32 [32, 1024, 2048], P('day', None, 'lon'), may hold values from 0.5 to 12
- counts: int32 [32, 1024, 2048], P('day', None, 'lon'), may hold values from 0 to 7
- land: int32 [32, 1024, 2048], P('day', None, 'lon'), may hold values 0 or 1
Outputs:
- step: float32 [32, 1024, 2048], P('day', None, 'lon')
- residual: float32 [32, 1024, 2048], P('day', None, 'lon')
All inputs are finite; a program needn't handle non-finite values. No bound on the sum of `land` on one device may be relied on, other than what follows from the above.
Results may differ from a plain program's by a relative error of at most 0.00023.
Values sent between devices are 32-bit elements; how exact they have to be, the bound alone decides.
A program may use at most 64 MiB of HBM per device.

v0:
```python
import jax
import jax.numpy as jnp
from jax import lax
from jax.sharding import PartitionSpec as P

ITERS = 2


prior_scale = 0.02


def padded(block, sides, width):
    for axis, dim in sides:
        count = lax.axis_size(axis)
        forward = [(i, i + 1) for i in range(count - 1)]
        forward.append((count - 1, 0))
        backward = [(target, source) for source, target in forward]
        low = lax.ppermute(
            lax.slice_in_dim(block, block.shape[dim] - width, None, axis=dim), axis, forward
        )
        high = lax.ppermute(lax.slice_in_dim(block, 0, width, axis=dim), axis, backward)
        block = jnp.concatenate([low, block, high], axis=dim)
    return block


def sweep_local(wide, range_sq):
    center = wide[1:-1, :, 1:-1]
    lat_pad = jnp.pad(center, ((0, 0), (1, 1), (0, 0)))
    beside = wide[2:, :, 1:-1] + wide[:-2, :, 1:-1]
    beside = beside + wide[1:-1, :, 2:] + wide[1:-1, :, :-2]
    beside = beside + lat_pad[:, 2:] + lat_pad[:, :-2]
    return (range_sq + 6.0) * center - beside


def sweep_once(field, range_sq):
    wide = padded(field, (("lon", 2), ("day", 0)), 1)
    return sweep_local(wide, range_sq)


def precond_product(residual, scaled):
    return lax.psum(jnp.sum(residual * scaled), ("lon", "day"))


def per_device(latent, range_sq, counts, land):
    mask = land.astype(jnp.float32)
    weight = mask * jnp.exp(latent)

    def apply_q(field):
        outer = sweep_once(sweep_once(field, range_sq), range_sq)
        return prior_scale * outer

    lat_rows = latent.shape[1]
    rows = jnp.arange(lat_rows).reshape(1, lat_rows, 1)
    neighbours = 6.0 - (rows == 0).astype(jnp.float32) - (rows == lat_rows - 1).astype(jnp.float32)
    precond = prior_scale * ((range_sq + 6.0) ** 2 + neighbours) + weight
    residual = -(apply_q(latent) + weight - mask * counts.astype(jnp.float32))
    step = jnp.zeros_like(latent)
    scaled = residual / precond
    direction = scaled
    rz_now = precond_product(residual, scaled)
    for turn in range(ITERS):
        image = apply_q(direction) + weight * direction
        alpha = rz_now / lax.psum(jnp.sum(direction * image), ("lon", "day"))
        step = step + alpha * direction
        residual = residual - alpha * image
        if turn + 1 < ITERS:
            scaled = residual / precond
            rz_next = precond_product(residual, scaled)
            direction = scaled + rz_next / rz_now * direction
            rz_now = rz_next
    return (step, residual)


def solution(mesh):
    in_specs = (
        P("day", None, "lon"),
        P("day", None, "lon"),
        P("day", None, "lon"),
        P("day", None, "lon"),
    )
    out_specs = (P("day", None, "lon"), P("day", None, "lon"))
    return jax.shard_map(
        per_device, mesh=mesh, in_specs=in_specs, out_specs=out_specs, check_vma=False
    )
```

profile of v0, /device:TPU:1, one launch (start us, length us, event | category | flops | bytes accessed | tf_op | source)
XLA Modules:
  0.0 371.4 jit_solution(10580727101622157870)
XLA Ops:
  0.6 4.2 %fusion.54 = (f32[4,1024,1]{2,1,0:T(8,128)S(1)}, f32[4,1024,1]{2,1,0:T(8,128)}) fusion(f32[4,1024,128]{2,1,0:T(8,128)} %param.4), kind=kLoop, calls=%fused_computation.142 | loop fusion | bytes 65536 | tf_op jit(solution)/shard_map/slice | solution.py:21
  4.8 2.2 copy.53
  7.0 2.5 collective-permute-start
  9.5 0.6 copy.54
  10.1 4.6 %collective-permute-start.1 = (f32[4,1024,1]{1,0,2:T(4,128)S(1)}, f32[4,1024,1]{1,0,2:T(4,128)S(1)}, u32[]{:S(2)}, u32[]{:S(2)}) collective-permute-start(f32[4,1024,1]{1,0,2:T(4,128)S(1)} %copy.54), channel_id=1, source_target_pairs={{8,0},{16,8},{24,16},{32,24},{40,32},{48,40},{56,48},{64,56},{72,6... | collective-permute-start | bytes 49160 | tf_op jit(solution)/shard_map/ppermute | solution.py:21
  14.8 1.9 copy.7
  16.8 1.1 pad_maximum_fusion.65
  17.9 1.0 collective-permute-start.2
  18.9 1.4 collective-permute-start.3
  20.3 1.9 copy.6
  22.2 5.6 %collective-permute-done.2 = f32[1,1024,130]{1,2,0:T(8,128)S(1)} collective-permute-done((f32[1,1024,130]{1,2,0:T(8,128)}, f32[1,1024,130]{1,2,0:T(8,128)S(1)}, u32[]{:S(2)}, u32[]{:S(2)}) %collective-permute-start.2) | collective-permute-done | bytes 532512 | tf_op jit(solution)/shard_map/ppermute | solution.py:21
  27.8 7.8 %fusion.2 = f32[4,1024,128]{1,2,0:T(8,128)S(1)} fusion(f32[4,1024,128]{1,2,0:T(8,128)} %copy-done.4, f32[4,1024,1]{1,2,0:T(1,128)S(1)} %copy.10, f32[4,1024,1]{1,2,0:T(1,128)S(1)} %copy.12, f32[1,1024,130]{1,2,0:T(8,128)} %collective-permute-done.3, f32[1,1024,130]{1,2,0:T(8,128)S(1)} %collective-permute-done.2, f32[4,1024,128]{1,2,0:T(8,128)S(1)} %copy.6), kind=kLoop, calls=%fused_computation.14 | loop fusion | flops 8388608 | bytes 7389184 | tf_op jit(solution)/shard_map/sub | solution.py:32
  35.6 0.1 collective-permute-start.4
  35.7 4.8 %collective-permute-start.5 = (f32[4,1024,1]{1,0,2:T(4,128)S(1)}, f32[4,1024,1]{1,0,2:T(4,128)S(1)}, u32[]{:S(2)}, u32[]{:S(2)}) collective-permute-start(f32[4,1024,1]{1,0,2:T(4,128)S(1)} %copy.19), channel_id=1, source_target_pairs={{8,0},{16,8},{24,16},{32,24},{40,32},{48,40},{56,48},{64,56},{72,6... | collective-permute-start | bytes 49160 | tf_op jit(solution)/shard_map/ppermute | solution.py:21
  40.5 1.1 collective-permute-done.4
  41.7 1.2 pad_maximum_fusion.62
  42.9 4.4 %collective-permute-start.6 = (f32[1,1024,130]{1,2,0:T(8,128)}, f32[1,1024,130]{1,2,0:T(8,128)S(1)}, u32[]{:S(2)}, u32[]{:S(2)}) collective-permute-start(f32[1,1024,130]{1,2,0:T(8,128)} %get-tuple-element.24), channel_id=1, source_target_pairs={{1,0},{2,1},{3,2},{4,3},{5,4},{6,5},{7,6},{0,7},{9,8},{10,9},{11,1... | collective-permute-start | bytes 1597448 | tf_op jit(solution)/shard_map/ppermute | solution.py:21
  47.3 2.9 copy.26
  50.2 2.9 copy.24
  53.1 0.2 collective-permute-done.6
  53.3 0.8 collective-permute-done.7
  54.1 9.8 %fusion.45 = (f32[4,1024,128]{1,2,0:T(8,128)S(1)}, f32[4,1024,128]{1,2,0:T(8,128)S(1)}, f32[4,1024,128]{1,2,0:T(8,128)S(1)}) fusion(f32[1024]{0:T(1024)S(1)} %convert_subtract_fusion, f32[4,1024,128]{1,2,0:T(8,128)S(1)} %copy.6, s32[4,1024,128]{1,2,0:T(8,128)} %copy.26, s32[4,1024,128]{1,2,0:T(8,128)} %copy.24, f32[4,1024,128]{1,2,0:T(8,128)} %copy-done.5, ...), kind=kLoop, calls=%fused_computation.133 | loop fusion | flops 15204352 | bytes 17879040 | tf_op jit(solution)/shard_map/div | solution.py:58
  63.9 0.0 copy-start.2
  63.9 0.0 copy-start.6
  64.0 0.1 collective-permute-start.8
  64.1 5.1 %collective-permute-start.9 = (f32[4,1024,1]{1,0,2:T(4,128)S(1)}, f32[4,1024,1]{1,0,2:T(4,128)S(1)}, u32[]{:S(2)}, u32[]{:S(2)}) collective-permute-start(f32[4,1024,1]{1,0,2:T(4,128)S(1)} %copy.28), channel_id=1, source_target_pairs={{8,0},{16,8},{24,16},{32,24},{40,32},{48,40},{56,48},{64,56},{72,6... | collective-permute-start | bytes 49160 | tf_op jit(solution)/shard_map/ppermute | solution.py:21
  69.2 1.0 collective-permute-done.8
  70.3 0.1 pad_maximum_fusion.59
  70.4 4.5 %collective-permute-start.10 = (f32[1,1024,130]{1,2,0:T(8,128)S(1)}, f32[1,1024,130]{1,2,0:T(8,128)S(1)}, u32[]{:S(2)}, u32[]{:S(2)}) collective-permute-start(f32[1,1024,130]{1,2,0:T(8,128)S(1)} %get-tuple-element.22), channel_id=1, source_target_pairs={{1,0},{2,1},{3,2},{4,3},{5,4},{6,5},{7,6},{0,7},{9,8},{10,9},{11,1... | collective-permute-start | bytes 1597448 | tf_op jit(solution)/shard_map/ppermute | solution.py:21
  74.9 6.3 %collective-permute-done.10 = f32[1,1024,130]{1,2,0:T(8,128)S(1)} collective-permute-done((f32[1,1024,130]{1,2,0:T(8,128)S(1)}, f32[1,1024,130]{1,2,0:T(8,128)S(1)}, u32[]{:S(2)}, u32[]{:S(2)}) %collective-permute-start.10) | collective-permute-done | bytes 532512 | tf_op jit(solution)/shard_map/ppermute | solution.py:21
  81.2 0.2 collective-permute-done.11
  81.3 3.2 fusion.12
  84.6 0.1 collective-permute-start.12
  84.7 5.3 %collective-permute-start.13 = (f32[4,1024,1]{1,0,2:T(4,128)S(1)}, f32[4,1024,1]{1,0,2:T(4,128)S(1)}, u32[]{:S(2)}, u32[]{:S(2)}) collective-permute-start(f32[4,1024,1]{1,0,2:T(4,128)S(1)} %copy.34), channel_id=1, source_target_pairs={{8,0},{16,8},{24,16},{32,24},{40,32},{48,40},{56,48},{64,56},{72,6... | collective-permute-start | bytes 49160 | tf_op jit(solution)/shard_map/ppermute | solution.py:21
  90.0 0.9 collective-permute-done.12
  90.9 0.1 pad_maximum_fusion.56
  91.0 4.6 %collective-permute-start.14 = (f32[1,1024,130]{1,2,0:T(8,128)S(1)}, f32[1,1024,130]{1,2,0:T(8,128)S(1)}, u32[]{:S(2)}, u32[]{:S(2)}) collective-permute-start(f32[1,1024,130]{1,2,0:T(8,128)S(1)} %get-tuple-element.20), channel_id=1, source_target_pairs={{1,0},{2,1},{3,2},{4,3},{5,4},{6,5},{7,6},{0,7},{9,8},{10,9},{11,1... | collective-permute-start | bytes 1597448 | tf_op jit(solution)/shard_map/ppermute | solution.py:21
  95.6 6.3 %collective-permute-done.14 = f32[1,1024,130]{1,2,0:T(8,128)S(1)} collective-permute-done((f32[1,1024,130]{1,2,0:T(8,128)S(1)}, f32[1,1024,130]{1,2,0:T(8,128)S(1)}, u32[]{:S(2)}, u32[]{:S(2)}) %collective-permute-start.14) | collective-permute-done | bytes 532512 | tf_op jit(solution)/shard_map/ppermute | solution.py:21
  101.9 0.2 collective-permute-done.15
  102.1 5.2 %multiply_reduce_fusion.2 = (f32[]{:T(128)}, f32[]{:T(128)}, f32[4,1024,128]{1,2,0:T(8,128)}) fusion(f32[4,1024,128]{1,2,0:T(8,128)S(1)} %get-tuple-element.13, f32[4,1024,128]{1,2,0:T(8,128)S(1)} %get-tuple-element.14, f32[4,1024,128]{1,2,0:T(8,128)S(1)} %get-tuple-element.15, f32[4,1024,128]{1,2,0:T(8,128)S(1)} %fusion.12, f32[4,1024,1]{1,2,0:T(1,128)S(1)} %copy.35, ...), kind=kLoop, calls=%fused_computation.110 | loop fusion | flops 12058622 | bytes 13680648 | tf_op jit(solution)/shard_map/reduce_sum | solution.py:63
  107.3 68.0 %all-reduce.6 = (f32[]{:T(128)}, f32[]{:T(128)}) all-reduce(f32[]{:T(128)} %get-tuple-element.5, f32[]{:T(128)} %get-tuple-element.4), channel_id=1, replica_groups=mesh['lon'=16,'day'=8] {'lon','day'}, use_global_device_ids=true, to_apply=%region_1.2 | all-reduce | flops 2 | bytes 16 | tf_op jit(solution)/shard_map/psum | solution.py:41
  176.6 5.8 %multiply_reduce_fusion.1 = (f32[]{:T(128)}, f32[4,1024,128]{1,2,0:T(8,128)}) fusion(f32[4,1024,128]{1,2,0:T(8,128)} %copy-done.2, f32[1024]{0:T(1024)S(1)} %convert_subtract_fusion, f32[4,1024,128]{1,2,0:T(8,128)S(1)} %copy.6, f32[4,1024,128]{1,2,0:T(8,128)} %copy-done.6, f32[4,1024,128]{1,2,0:T(8,128)} %get-tuple-element.12, f32[]{:T(128)S(6)} %div.16), kind=kLoop, calls=%fused_computation.108 | loop fusion | flops 5242879 | bytes 10489864 | tf_op jit(solution)/shard_map/reduce_sum | solution.py:41
  182.3 62.5 %psum.30 = f32[]{:T(128)} all-reduce(f32[]{:T(128)} %get-tuple-element.10), channel_id=1, replica_groups=mesh['lon'=16,'day'=8] {'lon','day'}, use_global_device_ids=true, to_apply=%region_5.6 | all-reduce | flops 1 | bytes 8 | tf_op jit(solution)/shard_map/psum | solution.py:41
  246.2 3.9 %multiply_add_fusion.1 = f32[4,1024,128]{1,2,0:T(8,128)S(1)} fusion(f32[4,1024,128]{1,2,0:T(8,128)} %copy-done, f32[]{:T(128)S(6)} %div.18, f32[4,1024,128]{1,2,0:T(8,128)} %get-tuple-element.11, f32[4,1024,128]{1,2,0:T(8,128)} %copy-done.2, f32[1024]{0:T(1024)S(1)} %convert_subtract_fusion, f32[4,1024,128]{1,2,0:T(8,128)S(1)} %copy.6), kind=kLoop, calls=%fused_computation.107 | loop fusion | flops 4194304 | bytes 10489860 | tf_op jit(solution)/shard_map/add | solution.py:69
  250.1 1.0 collective-permute-start.16
  251.1 3.9 %collective-permute-start.17 = (f32[4,1024,1]{1,0,2:T(4,128)S(1)}, f32[4,1024,1]{1,0,2:T(4,128)S(1)}, u32[]{:S(2)}, u32[]{:S(2)}) collective-permute-start(f32[4,1024,1]{1,0,2:T(4,128)S(1)} %copy.40), channel_id=1, source_target_pairs={{8,0},{16,8},{24,16},{32,24},{40,32},{48,40},{56,48},{64,56},{72,6... | collective-permute-start | bytes 49160 | tf_op jit(solution)/shard_map/ppermute | solution.py:21
  255.0 1.1 collective-permute-done.16
  256.2 0.1 pad_maximum_fusion.53
  256.3 1.7 collective-permute-start.18
  258.0 1.0 collective-permute-start.19
  259.1 7.5 %collective-permute-done.18 = f32[1,1024,130]{1,2,0:T(8,128)S(1)} collective-permute-done((f32[1,1024,130]{1,2,0:T(8,128)S(1)}, f32[1,1024,130]{1,2,0:T(8,128)S(1)}, u32[]{:S(2)}, u32[]{:S(2)}) %collective-permute-start.18) | collective-permute-done | bytes 532512 | tf_op jit(solution)/shard_map/ppermute | solution.py:21
  266.6 3.2 fusion.20
  269.8 0.0 copy-start.3
  269.9 0.1 collective-permute-start.20
  270.0 5.1 %collective-permute-start.21 = (f32[4,1024,1]{1,0,2:T(4,128)S(1)}, f32[4,1024,1]{1,0,2:T(4,128)S(1)}, u32[]{:S(2)}, u32[]{:S(2)}) collective-permute-start(f32[4,1024,1]{1,0,2:T(4,128)S(1)} %copy.46), channel_id=1, source_target_pairs={{8,0},{16,8},{24,16},{32,24},{40,32},{48,40},{56,48},{64,56},{72,6... | collective-permute-start | bytes 49160 | tf_op jit(solution)/shard_map/ppermute | solution.py:21
  275.1 1.0 collective-permute-done.20
  276.2 0.1 pad_maximum_fusion.50
  276.3 3.3 collective-permute-start.22
  279.6 6.6 %collective-permute-done.22 = f32[1,1024,130]{1,2,0:T(8,128)S(1)} collective-permute-done((f32[1,1024,130]{1,2,0:T(8,128)S(1)}, f32[1,1024,130]{1,2,0:T(8,128)S(1)}, u32[]{:S(2)}, u32[]{:S(2)}) %collective-permute-start.22) | collective-permute-done | bytes 532512 | tf_op jit(solution)/shard_map/ppermute | solution.py:21
  286.2 5.1 %multiply_reduce_fusion = (f32[]{:T(128)}, f32[4,1024,128]{1,2,0:T(8,128)}) fusion(f32[4,1024,128]{1,2,0:T(8,128)S(1)} %multiply_add_fusion.1, f32[4,1024,128]{1,2,0:T(8,128)S(1)} %copy-done.3, f32[4,1024,128]{1,2,0:T(8,128)S(1)} %fusion.20, f32[4,1024,1]{1,2,0:T(1,128)S(1)} %copy.47, f32[4,1024,1]{1,2,0:T(1,128)S(1)} %copy.48, ...), kind=kLoop, calls=%fused_computation.106 | loop fusion | flops 11010047 | bytes 11583492 | tf_op jit(solution)/shard_map/reduce_sum | solution.py:63
  291.3 67.8 %psum.31 = f32[]{:T(128)} all-reduce(f32[]{:T(128)} %get-tuple-element.8), channel_id=1, replica_groups=mesh['lon'=16,'day'=8] {'lon','day'}, use_global_device_ids=true, to_apply=%region_7.8 | all-reduce | flops 1 | bytes 8 | tf_op jit(solution)/shard_map/psum | solution.py:63
  360.5 6.2 %multiply_subtract_fusion = (f32[4,1024,128]{1,2,0:T(8,128)}, f32[4,1024,128]{1,2,0:T(8,128)S(1)}) fusion(f32[4,1024,128]{1,2,0:T(8,128)} %get-tuple-element.11, f32[4,1024,128]{1,2,0:T(8,128)} %get-tuple-element.9, f32[]{:T(128)S(6)} %div.19, f32[4,1024,128]{1,2,0:T(8,128)} %copy-done.1, f32[4,1024,128]{1,2,0:T(8,128)} %copy-done, f32[]{:T(128)S(6)} %div.16), kind=kLoop, calls=%fused_computation.104 | loop fusion | flops 2621440 | bytes 12582920 | tf_op jit(solution)/shard_map/sub | solution.py:65
  366.7 2.9 copy.52
  369.6 1.8 copy.51
  (53 shorter events, 0.5 us)
Async XLA Ops:
  7.0 9.7 %collective-permute-start = (f32[4,1024,1]{1,0,2:T(4,128)S(1)}, f32[4,1024,1]{1,0,2:T(4,128)S(1)}, u32[]{:S(2)}, u32[]{:S(2)}) collective-permute-start(f32[4,1024,1]{1,0,2:T(4,128)S(1)} %copy.53), channel_id=1, source_target_pairs={{0,8},{8,16},{16,24},{24,32},{32,40},{40,48},{48,56},{56,64},{64,7... | collective-permute-start | bytes 49160 | tf_op jit(solution)/shard_map/ppermute | solution.py:18
  10.1 6.6 %collective-permute-start.1 = (f32[4,1024,1]{1,0,2:T(4,128)S(1)}, f32[4,1024,1]{1,0,2:T(4,128)S(1)}, u32[]{:S(2)}, u32[]{:S(2)}) collective-permute-start(f32[4,1024,1]{1,0,2:T(4,128)S(1)} %copy.54), channel_id=1, source_target_pairs={{8,0},{16,8},{24,16},{32,24},{40,32},{48,40},{56,48},{64,56},{72,6... | collective-permute-start | bytes 49160 | tf_op jit(solution)/shard_map/ppermute | solution.py:21
  16.7 2.2 copy-start.4
  17.9 9.9 %collective-permute-start.2 = (f32[1,1024,130]{1,2,0:T(8,128)}, f32[1,1024,130]{1,2,0:T(8,128)S(1)}, u32[]{:S(2)}, u32[]{:S(2)}) collective-permute-start(f32[1,1024,130]{1,2,0:T(8,128)} %get-tuple-element.26), channel_id=1, source_target_pairs={{1,0},{2,1},{3,2},{4,3},{5,4},{6,5},{7,6},{0,7},{9,8},{10,9},{11,1... | collective-permute-start | bytes 1597448 | tf_op jit(solution)/shard_map/ppermute | solution.py:21
  18.9 8.9 %collective-permute-start.3 = (f32[1,1024,130]{1,2,0:T(8,128)S(1)}, f32[1,1024,130]{1,2,0:T(8,128)}, u32[]{:S(2)}, u32[]{:S(2)}) collective-permute-start(f32[1,1024,130]{1,2,0:T(8,128)S(1)} %get-tuple-element.27), channel_id=1, source_target_pairs={{0,1},{1,2},{2,3},{3,4},{4,5},{5,6},{6,7},{7,0},{8,9},{9,10},{10,1... | collective-permute-start | bytes 1597448 | tf_op jit(solution)/shard_map/ppermute | solution.py:18
  35.6 6.1 %copy-start.5 = (f32[4,1024,128]{1,2,0:T(8,128)}, f32[4,1024,128]{1,2,0:T(8,128)S(1)}, u32[]{:S(2)}) copy-start(f32[4,1024,128]{1,2,0:T(8,128)S(1)} %fusion.2) | copy-start | bytes 6291460
  35.6 6.0 %collective-permute-start.4 = (f32[4,1024,1]{1,0,2:T(4,128)S(1)}, f32[4,1024,1]{1,0,2:T(4,128)S(1)}, u32[]{:S(2)}, u32[]{:S(2)}) collective-permute-start(f32[4,1024,1]{1,0,2:T(4,128)S(1)} %copy.18), channel_id=1, source_target_pairs={{0,8},{8,16},{16,24},{24,32},{32,40},{40,48},{48,56},{56,64},{64,7... | collective-permute-start | bytes 49160 | tf_op jit(solution)/shard_map/ppermute | solution.py:18
  35.7 5.9 %collective-permute-start.5 = (f32[4,1024,1]{1,0,2:T(4,128)S(1)}, f32[4,1024,1]{1,0,2:T(4,128)S(1)}, u32[]{:S(2)}, u32[]{:S(2)}) collective-permute-start(f32[4,1024,1]{1,0,2:T(4,128)S(1)} %copy.19), channel_id=1, source_target_pairs={{8,0},{16,8},{24,16},{32,24},{40,32},{48,40},{56,48},{64,56},{72,6... | collective-permute-start | bytes 49160 | tf_op jit(solution)/shard_map/ppermute | solution.py:21
  42.9 10.4 %collective-permute-start.6 = (f32[1,1024,130]{1,2,0:T(8,128)}, f32[1,1024,130]{1,2,0:T(8,128)S(1)}, u32[]{:S(2)}, u32[]{:S(2)}) collective-permute-start(f32[1,1024,130]{1,2,0:T(8,128)} %get-tuple-element.24), channel_id=1, source_target_pairs={{1,0},{2,1},{3,2},{4,3},{5,4},{6,5},{7,6},{0,7},{9,8},{10,9},{11,1... | collective-permute-start | bytes 1597448 | tf_op jit(solution)/shard_map/ppermute | solution.py:21
  47.3 6.8 %collective-permute-start.7 = (f32[1,1024,130]{1,2,0:T(8,128)}, f32[1,1024,130]{1,2,0:T(8,128)S(1)}, u32[]{:S(2)}, u32[]{:S(2)}) collective-permute-start(f32[1,1024,130]{1,2,0:T(8,128)} %get-tuple-element.25), channel_id=1, source_target_pairs={{0,1},{1,2},{2,3},{3,4},{4,5},{5,6},{6,7},{7,0},{8,9},{9,10},{10,1... | collective-permute-start | bytes 1597448 | tf_op jit(solution)/shard_map/ppermute | solution.py:18
  63.9 38.2 %copy-start = (f32[4,1024,128]{1,2,0:T(8,128)}, f32[4,1024,128]{1,2,0:T(8,128)S(1)}, u32[]{:S(2)}) copy-start(f32[4,1024,128]{1,2,0:T(8,128)S(1)} %get-tuple-element.13) | copy-start | bytes 6291460
  63.9 38.2 %copy-start.2 = (f32[4,1024,128]{1,2,0:T(8,128)}, f32[4,1024,128]{1,2,0:T(8,128)S(1)}, u32[]{:S(2)}) copy-start(f32[4,1024,128]{1,2,0:T(8,128)S(1)} %get-tuple-element.15) | copy-start | bytes 6291460
  63.9 38.2 %copy-start.6 = (f32[4,1024,128]{1,2,0:T(8,128)}, f32[4,1024,128]{1,2,0:T(8,128)S(1)}, u32[]{:S(2)}) copy-start(f32[4,1024,128]{1,2,0:T(8,128)S(1)} %get-tuple-element.14) | copy-start | bytes 6291460
  64.0 6.2 %collective-permute-start.8 = (f32[4,1024,1]{1,0,2:T(4,128)S(1)}, f32[4,1024,1]{1,0,2:T(4,128)S(1)}, u32[]{:S(2)}, u32[]{:S(2)}) collective-permute-start(f32[4,1024,1]{1,0,2:T(4,128)S(1)} %copy.27), channel_id=1, source_target_pairs={{0,8},{8,16},{16,24},{24,32},{32,40},{40,48},{48,56},{56,64},{64,7... | collective-permute-start | bytes 49160 | tf_op jit(solution)/shard_map/ppermute | solution.py:18
  64.1 6.2 %collective-permute-start.9 = (f32[4,1024,1]{1,0,2:T(4,128)S(1)}, f32[4,1024,1]{1,0,2:T(4,128)S(1)}, u32[]{:S(2)}, u32[]{:S(2)}) collective-permute-start(f32[4,1024,1]{1,0,2:T(4,128)S(1)} %copy.28), channel_id=1, source_target_pairs={{8,0},{16,8},{24,16},{32,24},{40,32},{48,40},{56,48},{64,56},{72,6... | collective-permute-start | bytes 49160 | tf_op jit(solution)/shard_map/ppermute | solution.py:21
  70.4 10.8 %collective-permute-start.10 = (f32[1,1024,130]{1,2,0:T(8,128)S(1)}, f32[1,1024,130]{1,2,0:T(8,128)S(1)}, u32[]{:S(2)}, u32[]{:S(2)}) collective-permute-start(f32[1,1024,130]{1,2,0:T(8,128)S(1)} %get-tuple-element.22), channel_id=1, source_target_pairs={{1,0},{2,1},{3,2},{4,3},{5,4},{6,5},{7,6},{0,7},{9,8},{10,9},{11,1... | collective-permute-start | bytes 1597448 | tf_op jit(solution)/shard_map/ppermute | solution.py:21
  74.9 6.5 %collective-permute-start.11 = (f32[1,1024,130]{1,2,0:T(8,128)S(1)}, f32[1,1024,130]{1,2,0:T(8,128)S(1)}, u32[]{:S(2)}, u32[]{:S(2)}) collective-permute-start(f32[1,1024,130]{1,2,0:T(8,128)S(1)} %get-tuple-element.23), channel_id=1, source_target_pairs={{0,1},{1,2},{2,3},{3,4},{4,5},{5,6},{6,7},{7,0},{8,9},{9,10},{10,1... | collective-permute-start | bytes 1597448 | tf_op jit(solution)/shard_map/ppermute | solution.py:18
  84.6 6.3 %collective-permute-start.12 = (f32[4,1024,1]{1,0,2:T(4,128)S(1)}, f32[4,1024,1]{1,0,2:T(4,128)S(1)}, u32[]{:S(2)}, u32[]{:S(2)}) collective-permute-start(f32[4,1024,1]{1,0,2:T(4,128)S(1)} %copy.33), channel_id=1, source_target_pairs={{0,8},{8,16},{16,24},{24,32},{32,40},{40,48},{48,56},{56,64},{64,7... | collective-permute-start | bytes 49160 | tf_op jit(solution)/shard_map/ppermute | solution.py:18
  84.7 6.2 %collective-permute-start.13 = (f32[4,1024,1]{1,0,2:T(4,128)S(1)}, f32[4,1024,1]{1,0,2:T(4,128)S(1)}, u32[]{:S(2)}, u32[]{:S(2)}) collective-permute-start(f32[4,1024,1]{1,0,2:T(4,128)S(1)} %copy.34), channel_id=1, source_target_pairs={{8,0},{16,8},{24,16},{32,24},{40,32},{48,40},{56,48},{64,56},{72,6... | collective-permute-start | bytes 49160 | tf_op jit(solution)/shard_map/ppermute | solution.py:21
  91.0 10.9 %collective-permute-start.14 = (f32[1,1024,130]{1,2,0:T(8,128)S(1)}, f32[1,1024,130]{1,2,0:T(8,128)S(1)}, u32[]{:S(2)}, u32[]{:S(2)}) collective-permute-start(f32[1,1024,130]{1,2,0:T(8,128)S(1)} %get-tuple-element.20), channel_id=1, source_target_pairs={{1,0},{2,1},{3,2},{4,3},{5,4},{6,5},{7,6},{0,7},{9,8},{10,9},{11,1... | collective-permute-start | bytes 1597448 | tf_op jit(solution)/shard_map/ppermute | solution.py:21
  95.6 6.5 %collective-permute-start.15 = (f32[1,1024,130]{1,2,0:T(8,128)S(1)}, f32[1,1024,130]{1,2,0:T(8,128)S(1)}, u32[]{:S(2)}, u32[]{:S(2)}) collective-permute-start(f32[1,1024,130]{1,2,0:T(8,128)S(1)} %get-tuple-element.21), channel_id=1, source_target_pairs={{0,1},{1,2},{2,3},{3,4},{4,5},{5,6},{6,7},{7,0},{8,9},{9,10},{10,1... | collective-permute-start | bytes 1597448 | tf_op jit(solution)/shard_map/ppermute | solution.py:18
  250.1 36.1 %copy-start.1 = (f32[4,1024,128]{1,2,0:T(8,128)}, f32[4,1024,128]{1,2,0:T(8,128)S(1)}, u32[]{:S(2)}) copy-start(f32[4,1024,128]{1,2,0:T(8,128)S(1)} %multiply_add_fusion.1) | copy-start | bytes 6291460
  250.1 6.0 %collective-permute-start.16 = (f32[4,1024,1]{1,0,2:T(4,128)S(1)}, f32[4,1024,1]{1,0,2:T(4,128)S(1)}, u32[]{:S(2)}, u32[]{:S(2)}) collective-permute-start(f32[4,1024,1]{1,0,2:T(4,128)S(1)} %copy.39), channel_id=1, source_target_pairs={{0,8},{8,16},{16,24},{24,32},{32,40},{40,48},{48,56},{56,64},{64,7... | collective-permute-start | bytes 49160 | tf_op jit(solution)/shard_map/ppermute | solution.py:18
  251.1 5.0 %collective-permute-start.17 = (f32[4,1024,1]{1,0,2:T(4,128)S(1)}, f32[4,1024,1]{1,0,2:T(4,128)S(1)}, u32[]{:S(2)}, u32[]{:S(2)}) collective-permute-start(f32[4,1024,1]{1,0,2:T(4,128)S(1)} %copy.40), channel_id=1, source_target_pairs={{8,0},{16,8},{24,16},{32,24},{40,32},{48,40},{56,48},{64,56},{72,6... | collective-permute-start | bytes 49160 | tf_op jit(solution)/shard_map/ppermute | solution.py:21
  256.3 10.3 %collective-permute-start.18 = (f32[1,1024,130]{1,2,0:T(8,128)S(1)}, f32[1,1024,130]{1,2,0:T(8,128)S(1)}, u32[]{:S(2)}, u32[]{:S(2)}) collective-permute-start(f32[1,1024,130]{1,2,0:T(8,128)S(1)} %get-tuple-element.18), channel_id=1, source_target_pairs={{1,0},{2,1},{3,2},{4,3},{5,4},{6,5},{7,6},{0,7},{9,8},{10,9},{11,1... | collective-permute-start | bytes 1597448 | tf_op jit(solution)/shard_map/ppermute | solution.py:21
  258.0 8.5 %collective-permute-start.19 = (f32[1,1024,130]{1,2,0:T(8,128)S(1)}, f32[1,1024,130]{1,2,0:T(8,128)S(1)}, u32[]{:S(2)}, u32[]{:S(2)}) collective-permute-start(f32[1,1024,130]{1,2,0:T(8,128)S(1)} %get-tuple-element.19), channel_id=1, source_target_pairs={{0,1},{1,2},{2,3},{3,4},{4,5},{5,6},{6,7},{7,0},{8,9},{9,10},{10,1... | collective-permute-start | bytes 1597448 | tf_op jit(solution)/shard_map/ppermute | solution.py:18
  269.8 16.4 %copy-start.3 = (f32[4,1024,128]{1,2,0:T(8,128)S(1)}, f32[4,1024,128]{1,2,0:T(8,128)}, u32[]{:S(2)}) copy-start(f32[4,1024,128]{1,2,0:T(8,128)} %copy-done.2) | copy-start | bytes 6291460
  269.9 6.2 %collective-permute-start.20 = (f32[4,1024,1]{1,0,2:T(4,128)S(1)}, f32[4,1024,1]{1,0,2:T(4,128)S(1)}, u32[]{:S(2)}, u32[]{:S(2)}) collective-permute-start(f32[4,1024,1]{1,0,2:T(4,128)S(1)} %copy.45), channel_id=1, source_target_pairs={{0,8},{8,16},{16,24},{24,32},{32,40},{40,48},{48,56},{56,64},{64,7... | collective-permute-start | bytes 49160 | tf_op jit(solution)/shard_map/ppermute | solution.py:18
  270.0 6.2 %collective-permute-start.21 = (f32[4,1024,1]{1,0,2:T(4,128)S(1)}, f32[4,1024,1]{1,0,2:T(4,128)S(1)}, u32[]{:S(2)}, u32[]{:S(2)}) collective-permute-start(f32[4,1024,1]{1,0,2:T(4,128)S(1)} %copy.46), channel_id=1, source_target_pairs={{8,0},{16,8},{24,16},{32,24},{40,32},{48,40},{56,48},{64,56},{72,6... | collective-permute-start | bytes 49160 | tf_op jit(solution)/shard_map/ppermute | solution.py:21
  276.3 9.9 %collective-permute-start.22 = (f32[1,1024,130]{1,2,0:T(8,128)S(1)}, f32[1,1024,130]{1,2,0:T(8,128)S(1)}, u32[]{:S(2)}, u32[]{:S(2)}) collective-permute-start(f32[1,1024,130]{1,2,0:T(8,128)S(1)} %get-tuple-element.16), channel_id=1, source_target_pairs={{1,0},{2,1},{3,2},{4,3},{5,4},{6,5},{7,6},{0,7},{9,8},{10,9},{11,1... | collective-permute-start | bytes 1597448 | tf_op jit(solution)/shard_map/ppermute | solution.py:21
  279.6 6.6 %collective-permute-start.23 = (f32[1,1024,130]{1,2,0:T(8,128)S(1)}, f32[1,1024,130]{1,2,0:T(8,128)S(1)}, u32[]{:S(2)}, u32[]{:S(2)}) collective-permute-start(f32[1,1024,130]{1,2,0:T(8,128)S(1)} %get-tuple-element.17), channel_id=1, source_target_pairs={{0,1},{1,2},{2,3},{3,4},{4,5},{5,6},{6,7},{7,0},{8,9},{9,10},{10,1... | collective-permute-start | bytes 1597448 | tf_op jit(solution)/shard_map/ppermute | solution.py:18
where the time goes:
time: 372 us; the launch traced here: 371 us
  blocking collectives  198 us (53%)
  starting transfers between devices  54.5 us (15%)
  other arithmetic  53 us (14%)
  waiting for transfers between devices  38.8 us (10%)
  local copies, waits for them, and re-layouts  21.7 us (6%)
  between operations  5.01 us (1%)
    psum x2, blocking collectives, precond_product(): return lax.psum(jnp.sum(residual * scaled), ('lon', 'day'))  131 us
    psum x1, blocking collectives, per_device(): alpha = rz_now / lax.psum(jnp.sum(direction * image), ('lon', 'day'))  67.8 us
    ppermute x12, starting transfers between devices, padded(): lax.ppermute(lax.slice_in_dim(block, 0, width, axis=dim), axis, backward)  48.3 us
    ppermute x12, waiting for transfers between devices, padded(): lax.ppermute(lax.slice_in_dim(block, 0, width, axis=dim), axis, backward)  32.5 us
    unnamed x22, local copies, waits for them, and re-layouts  17.1 us
    sub x3, other arithmetic, sweep_local(): return (range_sq + 6.0) * center - beside  14.1 us
    reduce_sum x2, other arithmetic, per_device(): alpha = rz_now / lax.psum(jnp.sum(direction * image), ('lon', 'day'))  10.4 us
    div x1, other arithmetic, per_device(): scaled = residual / precond  9.77 us
  transfers between devices with their start and end apart: 24, of which 14 were waited for; matrix products, arithmetic and copies ran while one was open for 3% of the time, Pallas kernels for 0%

commit v1 on v0

v1 whole, which is shorter than its diff:
```python
import functools

import jax
import jax.numpy as jnp
from jax import lax
from jax.experimental import pallas as pl
from jax.experimental.pallas import tpu as pltpu
from jax.sharding import PartitionSpec as P

ROUNDS = 3
SCALE = 0.02
PAD = 8
GROUP = 8
CHUNK = 128
BLOCK = 32
MESH = pl.DeviceIdType.MESH


def kernel(
    names, n_day, n_lon,
    lat_h, rs_h, cnt_h, land_h, step_h, res_h,
    latp, rs6, cnt, land, weight, inv, p0p, up, r0, q0, sres, kv0, kv1, kv2,
    psend, vrecv, precv, csend, crecv, redsend, redrecv,
    plane_ss, plane_rs, col_ss, col_rs, red_ss, red_rs, in_sem, out_sem,
):
    days, lats, lons = rs6.shape
    last = days - 1
    chunks = lats // CHUNK
    groups = CHUNK // GROUP
    blocks = CHUNK // BLOCK
    per_block = BLOCK // GROUP
    me_d = lax.axis_index("day")
    me_l = lax.axis_index("lon")

    def device(day, lon):
        where = {"day": day, "lon": lon}
        return tuple(where[n] for n in names)

    day_peer = [device(lax.rem(me_d + k, n_day), me_l) for k in range(n_day)]
    lon_peer = [device(me_d, lax.rem(me_l + k, n_lon)) for k in range(n_lon)]
    sides = (day_peer[n_day - 1], day_peer[1])
    beside = (lon_peer[n_lon - 1], lon_peer[1])

    body = pl.ds(PAD, lats)
    loads = [
        pltpu.make_async_copy(lat_h, latp.at[:, body], in_sem.at[0]),
        pltpu.make_async_copy(rs_h, rs6, in_sem.at[1]),
        pltpu.make_async_copy(land_h, land, in_sem.at[2]),
        pltpu.make_async_copy(cnt_h, cnt, in_sem.at[3]),
    ]
    for copy in loads:
        copy.start()

    barrier = pltpu.get_barrier_semaphore()
    for peer in day_peer[1:] + lon_peer[1:]:
        pl.semaphore_signal(barrier, inc=1, device_id=peer, device_id_type=MESH)
    pl.semaphore_wait(barrier, n_day + n_lon - 2)

    fields = (latp, p0p, up)
    kvs = (kv0, kv1, kv2)
    edges = (0, last)

    def plane(rnd, kind, c, side):
        rows = pl.ds(c * CHUNK, CHUNK)
        if kind == 0:
            if rnd == 0:
                src = lat_h.at[edges[side], rows]
            else:
                src = fields[rnd].at[edges[side], pl.ds(PAD + c * CHUNK, CHUNK)]
            dst = vrecv.at[rnd, 1 - side, rows]
        else:
            src = psend.at[rnd, side, rows]
            dst = precv.at[rnd, 1 - side, rows]
        return pltpu.make_async_remote_copy(
            src_ref=src, dst_ref=dst,
            send_sem=plane_ss.at[rnd, kind, c, side], recv_sem=plane_rs.at[rnd, kind, c, 1 - side],
            device_id=sides[side], device_id_type=MESH,
        )

    def column(rnd, kind, c, side):
        return pltpu.make_async_remote_copy(
            src_ref=csend.at[rnd, kind, c], dst_ref=crecv.at[rnd, kind, c, 1 - side],
            send_sem=col_ss.at[rnd, kind, c, side], recv_sem=col_rs.at[rnd, kind, c, 1 - side],
            device_id=beside[side], device_id_type=MESH,
        )

    def start_both(copy, rnd, kind, c):
        copy(rnd, kind, c, 0).start()
        copy(rnd, kind, c, 1).start()

    def wait_both(copy, rnd, kind, c):
        copy(rnd, kind, c, 0).wait_recv()
        copy(rnd, kind, c, 1).wait_recv()

    def first_planes(c, carry):
        start_both(plane, 0, 0, c)
        return carry

    lax.fori_loop(0, chunks, first_planes, 0)

    lane = lax.broadcasted_iota(jnp.int32, (GROUP, lons), 1)
    pair = ((lane + 1) & (lons - 1)) >> 1
    lane_block = lax.broadcasted_iota(jnp.int32, (BLOCK, lons), 1)
    at_low = lane_block == 0
    at_high = lane_block == lons - 1
    even = (lane & 1) == 0
    zeros = jnp.zeros((GROUP, lons), jnp.float32)

    def gather(acc, tile, d, b):
        for k in range(per_block):
            j = d * groups + b * per_block + k
            acc = jnp.where(pair == j, pltpu.roll(tile[k * GROUP:(k + 1) * GROUP], 2 * j, 1), acc)
        return acc

    def outer_columns(rnd, kind, c):
        low = crecv[rnd, kind, c, 0]
        high = crecv[rnd, kind, c, 1]
        return jnp.where(even, pltpu.roll(low, 1, 1), pltpu.roll(high, lons - 1, 1))

    def along_lon(x, cols, d, b):
        outer = jnp.concatenate(
            [pltpu.roll(cols, (0 - 2 * (d * groups + b * per_block + k)) & (lons - 1), 1) for k in range(per_block)], axis=0
        )
        return jnp.where(at_low, outer, pltpu.roll(x, 1, 1)) + jnp.where(at_high, outer, pltpu.roll(x, lons - 1, 1))

    def own_part(ref, cols, row, b):
        x = [ref[d, pl.ds(PAD + row, BLOCK)] for d in range(days)]
        out = []
        for d in range(days):
            near = ref[d, pl.ds(PAD - 1 + row, BLOCK)] + ref[d, pl.ds(PAD + 1 + row, BLOCK)]
            near = near + along_lon(x[d], cols, d, b)
            if d > 0:
                near = near + x[d - 1]
            if d < last:
                near = near + x[d + 1]
            out.append(rs6[d, pl.ds(row, BLOCK)] * x[d] - near)
        return out

    def send_columns(rnd, kind, c, acc):
        csend[rnd, kind, c] = acc
        start_both(column, rnd, kind, c)

    def first_k(rnd, c, total):
        wait_both(column, rnd, 0, c)
        cols = outer_columns(rnd, 0, c)
        field, kv = fields[rnd], kvs[rnd]

        def partial(b, carry):
            row = pl.multiple_of(c * CHUNK + b * BLOCK, BLOCK)
            out = own_part(field, cols, row, b)
            rows = pl.ds(row, BLOCK)
            psend[rnd, 0, rows] = out[0]
            psend[rnd, 1, rows] = out[last]
            for d in range(1, last):
                kv[d, pl.ds(PAD + row, BLOCK)] = out[d]
            return carry

        lax.fori_loop(0, blocks, partial, 0)
        start_both(plane, rnd, 1, c)
        wait_both(plane, rnd, 0, c)

        def complete(b, carry):
            acc, total = carry
            row = pl.multiple_of(c * CHUNK + b * BLOCK, BLOCK)
            rows = pl.ds(row, BLOCK)
            for d in range(days):
                if d == 0 or d == last:
                    side = 0 if d == 0 else 1
                    tile = psend[rnd, side, rows] - vrecv[rnd, side, rows]
                    kv[d, pl.ds(PAD + row, BLOCK)] = tile
                else:
                    tile = kv[d, pl.ds(PAD + row, BLOCK)]
                acc = gather(acc, tile, d, b)
                if rnd == 1:
                    p = field[d, pl.ds(PAD + row, BLOCK)]
                    total = total + fold(SCALE * tile * tile + weight[d, rows] * p * p)
            return acc, total

        acc, total = lax.fori_loop(0, blocks, complete, (zeros, total))
        send_columns(rnd, 1, c, acc)
        return total

    def fold(x):
        return sum(x[k * GROUP:(k + 1) * GROUP] for k in range(1, per_block)) + x[:GROUP]

    def second_k(rnd, c, total):
        wait_both(column, rnd, 1, c)
        wait_both(plane, rnd, 1, c)
        cols = outer_columns(rnd, 1, c)
        field, kv = fields[rnd], kvs[rnd]

        def rest(b, carry):
            acc, total = carry
            row = pl.multiple_of(c * CHUNK + b * BLOCK, BLOCK)
            rows = pl.ds(row, BLOCK)
            wide = pl.ds(PAD + row, BLOCK)
            out = own_part(kv, cols, row, b)
            out[0] = out[0] - (precv[rnd, 0, rows] - field[0, wide])
            out[last] = out[last] - (precv[rnd, 1, rows] - field[last, wide])
            for d in range(days):
                image = SCALE * out[d]
                if rnd == 0:
                    base = sres[d, rows]
                    residual = 0.0 - (image + base)
                    value = residual * inv[d, rows]
                    r0[d, rows] = residual
                    p0p[d, wide] = value
                    total = total + fold(residual * value)
                else:
                    image = image + weight[d, rows] * field[d, wide]
                    if rnd == 1:
                        value = image * inv[d, rows]
                        q0[d, rows] = image
                        up[d, wide] = value
                    else:
                        sres[d, rows] = image
                if rnd < ROUNDS - 1:
                    acc = gather(acc, value, d, b)
            return acc, total

        acc, total = lax.fori_loop(0, blocks, rest, (zeros, total))
        if rnd < ROUNDS - 1:
            start_both(plane, rnd + 1, 0, c)
            send_columns(rnd + 1, 0, c, acc)
        return total

    count = redsend.shape[2]

    def peer_copy(which, stage, k):
        peers = (lon_peer, day_peer)[stage]
        return pltpu.make_async_remote_copy(
            src_ref=redsend.at[which, stage], dst_ref=redrecv.at[which, stage, k],
            send_sem=red_ss.at[which, stage, k], recv_sem=red_rs.at[which, stage, k],
            device_id=peers[k], device_id_type=MESH,
        )

    def reduce_start(which, stage, values):
        for i, v in enumerate(values):
            redsend[which, stage, i] = v
        for k in range(1, (n_lon, n_day)[stage]):
            peer_copy(which, stage, k).start()

    def reduce_wait(which, stage, used):
        n = (n_lon, n_day)[stage]
        for k in range(1, n):
            peer_copy(which, stage, k).wait_recv()
        out = []
        for i in range(used):
            total = redsend[which, stage, i]
            for k in range(1, n):
                total = total + redrecv[which, stage, k, i]
            out.append(total)
        return out

    def scalar(x):
        return jnp.sum(x)

    loads[0].wait()
    for ref in (latp, p0p, up, kv0, kv1, kv2):
        for d in range(days):
            ref[d, pl.ds(0, PAD)] = zeros
            ref[d, pl.ds(PAD + lats, PAD)] = zeros

    def first_columns(c, carry):
        def step(b, acc):
            row = pl.multiple_of(c * CHUNK + b * BLOCK, BLOCK)
            for d in range(days):
                acc = gather(acc, latp[d, pl.ds(PAD + row, BLOCK)], d, b)
            return acc

        send_columns(0, 0, c, lax.fori_loop(0, blocks, step, zeros))
        return carry

    lax.fori_loop(0, chunks, first_columns, 0)

    for copy in loads[1:]:
        copy.wait()

    def prepare(b, carry):
        row = pl.multiple_of(b * BLOCK, BLOCK)
        rows = pl.ds(row, BLOCK)
        at = row + lax.broadcasted_iota(jnp.int32, (BLOCK, lons), 0)
        near = 6.0 - jnp.where(at == 0, 1.0, 0.0) - jnp.where(at == lats - 1, 1.0, 0.0)
        for d in range(days):
            mask = land[d, rows].astype(jnp.float32)
            w = mask * jnp.exp(latp[d, pl.ds(PAD + row, BLOCK)])
            diag = rs6[d, rows] + 6.0
            rs6[d, rows] = diag
            weight[d, rows] = w
            inv[d, rows] = 1.0 / (SCALE * (diag * diag + near) + w)
            sres[d, rows] = w - mask * cnt[d, rows].astype(jnp.float32)
        return carry

    lax.fori_loop(0, lats // BLOCK, prepare, 0)

    m0 = m1 = zeros
    for rnd in range(ROUNDS):
        m1 = lax.fori_loop(0, chunks, functools.partial(first_k, rnd), m1)
        if rnd == 1:
            reduce_start(0, 0, [m0, m1])
        if rnd == 2:
            s0, s1 = [scalar(v) for v in reduce_wait(0, 1, 2)]
            rz0 = s0
            a0 = jnp.full((BLOCK, lons), s0) / jnp.full((BLOCK, lons), s1)

            def sums(b, carry):
                rz, zq, zz = carry
                row = pl.multiple_of(b * BLOCK, BLOCK)
                rows = pl.ds(row, BLOCK)
                wide = pl.ds(PAD + row, BLOCK)
                for d in range(days):
                    q = q0[d, rows]
                    z = p0p[d, wide] - a0 * up[d, wide]
                    kz = kv1[d, wide] - a0 * kv2[d, wide]
                    rz = rz + fold((r0[d, rows] - a0 * q) * z)
                    zq = zq + fold(z * q)
                    zz = zz + fold(SCALE * kz * kz + weight[d, rows] * z * z)
                return rz, zq, zz

            reduce_start(1, 0, lax.fori_loop(0, lats // BLOCK, sums, (zeros, zeros, zeros)))
        turn = functools.partial(second_k, rnd)
        if rnd == 0:
            m0 = lax.fori_loop(0, chunks, turn, m0)
        else:
            split = chunks - 2
            lax.fori_loop(0, split, turn, zeros)
            reduce_start(rnd - 1, 1, reduce_wait(rnd - 1, 0, (2, 3)[rnd - 1]))
            lax.fori_loop(split, chunks, turn, zeros)

    t0, t1, t2 = [scalar(v) for v in reduce_wait(1, 1, 3)]
    wide_of = lambda v: jnp.full((BLOCK, lons), v)
    rz1, zq, zz = wide_of(t0), wide_of(t1), wide_of(t2)
    beta = rz1 / wide_of(rz0)
    a1 = rz1 / (zz + 2.0 * beta * zq + beta * beta * wide_of(s1))
    coef_p = a0 + a1 * (1.0 + beta)
    coef_u = a0 * a1

    def out_copies(c):
        rows = pl.ds(c * CHUNK, CHUNK)
        return (
            pltpu.make_async_copy(q0.at[:, rows], step_h.at[:, rows], out_sem.at[0, c]),
            pltpu.make_async_copy(sres.at[:, rows], res_h.at[:, rows], out_sem.at[1, c]),
        )

    def finish(c, carry):
        def one(b, carry):
            row = pl.multiple_of(c * CHUNK + b * BLOCK, BLOCK)
            rows = pl.ds(row, BLOCK)
            wide = pl.ds(PAD + row, BLOCK)
            for d in range(days):
                q = q0[d, rows]
                sres[d, rows] = r0[d, rows] - coef_p * q + coef_u * sres[d, rows]
                q0[d, rows] = coef_p * p0p[d, wide] - coef_u * up[d, wide]
            return carry

        lax.fori_loop(0, blocks, one, 0)
        for copy in out_copies(c):
            copy.start()
        return carry

    lax.fori_loop(0, chunks, finish, 0)

    def drain(c, carry):
        for copy in out_copies(c):
            copy.wait()
        for rnd in range(ROUNDS):
            for kind in range(2):
                for side in range(2):
                    plane(rnd, kind, c, side).wait_send()
                    column(rnd, kind, c, side).wait_send()
        return carry

    lax.fori_loop(0, chunks, drain, 0)
    for which in range(2):
        for stage in range(2):
            for k in range(1, (n_lon, n_day)[stage]):
                peer_copy(which, stage, k).wait_send()


def solution(mesh):
    names = tuple(mesh.axis_names)
    n_day, n_lon = mesh.shape["day"], mesh.shape["lon"]
    spec = P("day", None, "lon")

    def per_device(latent, range_sq, counts, land):
        days, lats, lons = latent.shape
        chunks = lats // CHUNK
        f32 = jnp.float32
        whole = (days, lats, lons)
        padded = (days, lats + 2 * PAD, lons)
        vmem = pltpu.VMEM
        dma = pltpu.SemaphoreType.DMA
        return pl.pallas_call(
            functools.partial(kernel, names, n_day, n_lon),
            out_shape=[jax.ShapeDtypeStruct(whole, f32)] * 2,
            in_specs=[pl.BlockSpec(memory_space=pl.ANY)] * 4,
            out_specs=[pl.BlockSpec(memory_space=pl.ANY)] * 2,
            scratch_shapes=[
                vmem(padded, f32), vmem(whole, f32), vmem(whole, jnp.int32), vmem(whole, jnp.int32),
                vmem(whole, f32), vmem(whole, f32), vmem(padded, f32), vmem(padded, f32),
                vmem(whole, f32), vmem(whole, f32), vmem(whole, f32),
                vmem(padded, f32), vmem(padded, f32), vmem(padded, f32),
                vmem((ROUNDS, 2, lats, lons), f32), vmem((ROUNDS, 2, lats, lons), f32),
                vmem((ROUNDS, 2, lats, lons), f32),
                vmem((ROUNDS, 2, chunks, GROUP, lons), f32), vmem((ROUNDS, 2, chunks, 2, GROUP, lons), f32),
                vmem((2, 2, 3, GROUP, lons), f32), vmem((2, 2, n_lon, 3, GROUP, lons), f32),
                dma((ROUNDS, 2, chunks, 2)), dma((ROUNDS, 2, chunks, 2)),
                dma((ROUNDS, 2, chunks, 2)), dma((ROUNDS, 2, chunks, 2)),
                dma((2, 2, n_lon)), dma((2, 2, n_lon)), dma((4,)), dma((2, chunks)),
            ],
            compiler_params=pltpu.CompilerParams(
                collective_id=0, has_side_effects=True, vmem_limit_bytes=60 << 20
            ),
        )(latent, range_sq, counts, land)

    return jax.shard_map(per_device, mesh=mesh, in_specs=(spec,) * 4, out_specs=(spec, spec), check_vma=False)
```

time: 372 us -> 72.2 us (0.19)
  blocking collectives: 198 us -> 0 us
  Pallas kernels: 0 us -> 67 us
  starting transfers between devices: 54.5 us -> 0 us
  other arithmetic: 53 us -> 0 us
  waiting for transfers between devices: 38.8 us -> 0 us
  local copies, waits for them, and re-layouts: 21.7 us -> 4.52 us
  between operations: 5.01 us -> 0.65 us
    psum x3 -> x0, blocking collectives: 198 us -> none  [the longest x2 131 us: precond_product(): return lax.psum(jnp.sum(residual * scaled), ('lon', 'day'))]
    pallas_call x0 -> x1, Pallas kernels: none -> 67 us  [per_device(): pl.pallas_call(functools.partial(kernel, names, n_day, n_lon), out_shape=...]
    ppermute x24 -> x0, starting transfers between devices: 54.5 us -> none  [the longest x12 48.3 us: padded(): lax.ppermute(lax.slice_in_dim(block, 0, width, axis=dim), axis, backward)]
    ppermute x24 -> x0, waiting for transfers between devices: 38.8 us -> none  [the longest x12 32.5 us: padded(): lax.ppermute(lax.slice_in_dim(block, 0, width, axis=dim), axis, backward)]
    sub x5 -> x0, other arithmetic: 20.4 us -> none  [the longest x3 14.1 us: sweep_local(): return (range_sq + 6.0) * center - beside]
    reduce_sum x3 -> x0, other arithmetic: 16.1 us -> none  [the longest x2 10.4 us: per_device(): alpha = rz_now / lax.psum(jnp.sum(direction * image), ('lon', 'day'))]
    unnamed x22 -> x4, local copies, waits for them, and re-layouts: 17.1 us -> 4.52 us
    div x1 -> x0, other arithmetic: 9.77 us -> none  [per_device(): scaled = residual / precond]
  transfers between devices with their start and end apart: 24 -> 0, of which waited for: 14 -> 0; matrix products, arithmetic and copies ran while one was open for 3% -> 0% of each run, Pallas kernels for 0% -> 0%
where the time goes in v1:
time: 72.2 us; the launch traced here: 72.1 us
  Pallas kernels  67 us (93%)
  local copies, waits for them, and re-layouts  4.52 us (6%)
    pallas_call x1, Pallas kernels, per_device(): pl.pallas_call(functools.partial(kernel, names, n_day, n_lon), out_shape=...  67 us
    unnamed x4, local copies, waits for them, and re-layouts  4.52 us

profile of v1, /device:TPU:1, one launch (start us, length us, event | category | flops | bytes accessed | tf_op | source)
XLA Modules:
  0.0 72.1 jit_solution(3890576199776744016)
XLA Ops:
  0.6 67.0 %shard_map.59 = (f32[4,1024,128]{2,1,0:T(8,128)}, f32[4,1024,128]{2,1,0:T(8,128)}) custom-call(f32[4,1024,128]{2,1,0:T(8,128)} %lat_h.1, f32[4,1024,128]{2,1,0:T(8,128)} %rs_h.1, s32[4,1024,128]{2,1,0:T(8,128)} %cnt_h.1, s32[4,1024,128]{2,1,0:T(8,128)} %land_h.1), custom_call_target="tpu_custom_call" | custom-call | tf_op jit(solution)/shard_map/pallas_call | solution.py:393
  67.6 0.0 copy-start
  67.6 3.2 %copy.8 = f32[4,1024,128]{2,1,0:T(8,128)} copy(f32[4,1024,128]{2,1,0:T(8,128)} %get-tuple-element.4) | data formatting | bytes 4194304
  70.8 0.0 copy-done
  70.8 1.3 %copy.9 = f32[4,1024,128]{2,1,0:T(8,128)} copy(f32[4,1024,128]{2,1,0:T(8,128)S(1)} %copy-done) | data formatting | bytes 4194304
Async XLA Ops:
  67.6 3.2 %copy-start = (f32[4,1024,128]{2,1,0:T(8,128)S(1)}, f32[4,1024,128]{2,1,0:T(8,128)}, u32[]{:S(2)}) copy-start(f32[4,1024,128]{2,1,0:T(8,128)} %get-tuple-element.5) | copy-start | bytes 6291460

commit v2 on v1

--- a/solution.py
+++ b/solution.py
@@ -12,7 +12,8 @@
 PAD = 8
 GROUP = 8
 CHUNK = 128
-BLOCK = 32
+BLOCK = 128
+SMALL = 32
 MESH = pl.DeviceIdType.MESH
 
 
@@ -84,6 +85,11 @@
             device_id=beside[side], device_id_type=MESH,
         )
 
+    def unrolled(n, body, carry):
+        for i in range(n):
+            carry = body(i, carry)
+        return carry
+
     def start_both(copy, rnd, kind, c):
         copy(rnd, kind, c, 0).start()
         copy(rnd, kind, c, 1).start()
@@ -106,10 +112,11 @@
     even = (lane & 1) == 0
     zeros = jnp.zeros((GROUP, lons), jnp.float32)
 
-    def gather(acc, tile, d, b):
+    def gather(tile, d, b):
+        acc = zeros
         for k in range(per_block):
             j = d * groups + b * per_block + k
-            acc = jnp.where(pair == j, pltpu.roll(tile[k * GROUP:(k + 1) * GROUP], 2 * j, 1), acc)
+            acc = jnp.where(pair == j, pltpu.roll(tile[k * GROUP:(k + 1) * GROUP], (2 * j) % lons, 1), acc)
         return acc
 
     def outer_columns(rnd, kind, c):
@@ -119,7 +126,7 @@
 
     def along_lon(x, cols, d, b):
         outer = jnp.concatenate(
-            [pltpu.roll(cols, (0 - 2 * (d * groups + b * per_block + k)) & (lons - 1), 1) for k in range(per_block)], axis=0
+            [pltpu.roll(cols, (0 - 2 * (d * groups + b * per_block + k)) % lons, 1) for k in range(per_block)], axis=0
         )
         return jnp.where(at_low, outer, pltpu.roll(x, 1, 1)) + jnp.where(at_high, outer, pltpu.roll(x, lons - 1, 1))
 
@@ -155,7 +162,7 @@
                 kv[d, pl.ds(PAD + row, BLOCK)] = out[d]
             return carry
 
-        lax.fori_loop(0, blocks, partial, 0)
+        unrolled(blocks, partial, 0)
         start_both(plane, rnd, 1, c)
         wait_both(plane, rnd, 0, c)
 
@@ -170,18 +177,21 @@
                     kv[d, pl.ds(PAD + row, BLOCK)] = tile
                 else:
                     tile = kv[d, pl.ds(PAD + row, BLOCK)]
-                acc = gather(acc, tile, d, b)
+                acc = acc + gather(tile, d, b)
                 if rnd == 1:
                     p = field[d, pl.ds(PAD + row, BLOCK)]
                     total = total + fold(SCALE * tile * tile + weight[d, rows] * p * p)
             return acc, total
 
-        acc, total = lax.fori_loop(0, blocks, complete, (zeros, total))
+        acc, total = unrolled(blocks, complete, (zeros, total))
         send_columns(rnd, 1, c, acc)
         return total
 
     def fold(x):
-        return sum(x[k * GROUP:(k + 1) * GROUP] for k in range(1, per_block)) + x[:GROUP]
+        while x.shape[0] > GROUP:
+            half = x.shape[0] // 2
+            x = x[:half] + x[half:]
+        return x
 
     def second_k(rnd, c, total):
         wait_both(column, rnd, 1, c)
@@ -215,10 +225,10 @@
                     else:
                         sres[d, rows] = image
                 if rnd < ROUNDS - 1:
-                    acc = gather(acc, value, d, b)
+                    acc = acc + gather(value, d, b)
             return acc, total
 
-        acc, total = lax.fori_loop(0, blocks, rest, (zeros, total))
+        acc, total = unrolled(blocks, rest, (zeros, total))
         if rnd < ROUNDS - 1:
             start_both(plane, rnd + 1, 0, c)
             send_columns(rnd + 1, 0, c, acc)
@@ -265,10 +275,10 @@
         def step(b, acc):
             row = pl.multiple_of(c * CHUNK + b * BLOCK, BLOCK)
             for d in range(days):
-                acc = gather(acc, latp[d, pl.ds(PAD + row, BLOCK)], d, b)
+                acc = acc + gather(latp[d, pl.ds(PAD + row, BLOCK)], d, b)
             return acc
 
-        send_columns(0, 0, c, lax.fori_loop(0, blocks, step, zeros))
+        send_columns(0, 0, c, unrolled(blocks, step, zeros))
         return carry
 
     lax.fori_loop(0, chunks, first_columns, 0)
@@ -277,13 +287,13 @@
         copy.wait()
 
     def prepare(b, carry):
-        row = pl.multiple_of(b * BLOCK, BLOCK)
-        rows = pl.ds(row, BLOCK)
-        at = row + lax.broadcasted_iota(jnp.int32, (BLOCK, lons), 0)
+        row = pl.multiple_of(b * SMALL, SMALL)
+        rows = pl.ds(row, SMALL)
+        at = row + lax.broadcasted_iota(jnp.int32, (SMALL, lons), 0)
         near = 6.0 - jnp.where(at == 0, 1.0, 0.0) - jnp.where(at == lats - 1, 1.0, 0.0)
         for d in range(days):
             mask = land[d, rows].astype(jnp.float32)
-            w = mask * jnp.exp(latp[d, pl.ds(PAD + row, BLOCK)])
+            w = mask * jnp.exp(latp[d, pl.ds(PAD + row, SMALL)])
             diag = rs6[d, rows] + 6.0
             rs6[d, rows] = diag
             weight[d, rows] = w
@@ -291,7 +301,7 @@
             sres[d, rows] = w - mask * cnt[d, rows].astype(jnp.float32)
         return carry
 
-    lax.fori_loop(0, lats // BLOCK, prepare, 0)
+    lax.fori_loop(0, lats // SMALL, prepare, 0)
 
     m0 = m1 = zeros
     for rnd in range(ROUNDS):
@@ -301,13 +311,13 @@
         if rnd == 2:
             s0, s1 = [scalar(v) for v in reduce_wait(0, 1, 2)]
             rz0 = s0
-            a0 = jnp.full((BLOCK, lons), s0) / jnp.full((BLOCK, lons), s1)
+            a0 = jnp.full((SMALL, lons), s0) / jnp.full((SMALL, lons), s1)
 
             def sums(b, carry):
                 rz, zq, zz = carry
-                row = pl.multiple_of(b * BLOCK, BLOCK)
-                rows = pl.ds(row, BLOCK)
-                wide = pl.ds(PAD + row, BLOCK)
+                row = pl.multiple_of(b * SMALL, SMALL)
+                rows = pl.ds(row, SMALL)
+                wide = pl.ds(PAD + row, SMALL)
                 for d in range(days):
                     q = q0[d, rows]
                     z = p0p[d, wide] - a0 * up[d, wide]
@@ -317,7 +327,7 @@
                     zz = zz + fold(SCALE * kz * kz + weight[d, rows] * z * z)
                 return rz, zq, zz
 
-            reduce_start(1, 0, lax.fori_loop(0, lats // BLOCK, sums, (zeros, zeros, zeros)))
+            reduce_start(1, 0, lax.fori_loop(0, lats // SMALL, sums, (zeros, zeros, zeros)))
         turn = functools.partial(second_k, rnd)
         if rnd == 0:
             m0 = lax.fori_loop(0, chunks, turn, m0)
@@ -328,7 +338,7 @@
             lax.fori_loop(split, chunks, turn, zeros)
 
     t0, t1, t2 = [scalar(v) for v in reduce_wait(1, 1, 3)]
-    wide_of = lambda v: jnp.full((BLOCK, lons), v)
+    wide_of = lambda v: jnp.full((SMALL, lons), v)
     rz1, zq, zz = wide_of(t0), wide_of(t1), wide_of(t2)
     beta = rz1 / wide_of(rz0)
     a1 = rz1 / (zz + 2.0 * beta * zq + beta * beta * wide_of(s1))
@@ -344,16 +354,16 @@
 
     def finish(c, carry):
         def one(b, carry):
-            row = pl.multiple_of(c * CHUNK + b * BLOCK, BLOCK)
-            rows = pl.ds(row, BLOCK)
-            wide = pl.ds(PAD + row, BLOCK)
+            row = pl.multiple_of(c * CHUNK + b * SMALL, SMALL)
+            rows = pl.ds(row, SMALL)
+            wide = pl.ds(PAD + row, SMALL)
             for d in range(days):
                 q = q0[d, rows]
                 sres[d, rows] = r0[d, rows] - coef_p * q + coef_u * sres[d, rows]
                 q0[d, rows] = coef_p * p0p[d, wide] - coef_u * up[d, wide]
             return carry
 
-        lax.fori_loop(0, blocks, one, 0)
+        lax.fori_loop(0, CHUNK // SMALL, one, 0)
         for copy in out_copies(c):
             copy.start()
         return carry

time: 72.2 us -> 62.7 us (0.87)
  Pallas kernels: 67 us -> 57.4 us
    pallas_call x1, Pallas kernels: 67 us -> 57.4 us  [per_device(): pl.pallas_call(functools.partial(kernel, names, n_day, n_lon), out_shape=...]
where the time goes in v2:
time: 62.7 us; the launch traced here: 62.6 us
  Pallas kernels  57.4 us (92%)
  local copies, waits for them, and re-layouts  4.52 us (7%)
  between operations  0.65 us (1%)
    pallas_call x1, Pallas kernels, per_device(): pl.pallas_call(functools.partial(kernel, names, n_day, n_lon), out_shape=...  57.4 us
    unnamed x4, local copies, waits for them, and re-layouts  4.52 us

profile of v2, /device:TPU:1, one launch (start us, length us, event | category | flops | bytes accessed | tf_op | source)
XLA Modules:
  0.0 62.6 jit_solution(16736891110024794792)
XLA Ops:
  0.6 57.4 %shard_map.59 = (f32[4,1024,128]{2,1,0:T(8,128)}, f32[4,1024,128]{2,1,0:T(8,128)}) custom-call(f32[4,1024,128]{2,1,0:T(8,128)} %lat_h.1, f32[4,1024,128]{2,1,0:T(8,128)} %rs_h.1, s32[4,1024,128]{2,1,0:T(8,128)} %cnt_h.1, s32[4,1024,128]{2,1,0:T(8,128)} %land_h.1), custom_call_target="tpu_custom_call" | custom-call | tf_op jit(solution)/shard_map/pallas_call | solution.py:403
  58.1 0.0 copy-start
  58.1 3.2 %copy.8 = f32[4,1024,128]{2,1,0:T(8,128)} copy(f32[4,1024,128]{2,1,0:T(8,128)} %get-tuple-element.4) | data formatting | bytes 4194304
  61.3 0.0 copy-done
  61.3 1.3 %copy.9 = f32[4,1024,128]{2,1,0:T(8,128)} copy(f32[4,1024,128]{2,1,0:T(8,128)S(1)} %copy-done) | data formatting | bytes 4194304
Async XLA Ops:
  58.1 3.2 %copy-start = (f32[4,1024,128]{2,1,0:T(8,128)S(1)}, f32[4,1024,128]{2,1,0:T(8,128)}, u32[]{:S(2)}) copy-start(f32[4,1024,128]{2,1,0:T(8,128)} %get-tuple-element.5) | copy-start | bytes 6291460

commit v3 on v2

--- a/solution.py
+++ b/solution.py
@@ -13,16 +13,16 @@
 GROUP = 8
 CHUNK = 128
 BLOCK = 128
-SMALL = 32
+SMALL = 64
 MESH = pl.DeviceIdType.MESH
 
 
 def kernel(
     names, n_day, n_lon,
-    lat_h, rs_h, cnt_h, land_h, step_h, res_h,
-    latp, rs6, cnt, land, weight, inv, p0p, up, r0, q0, sres, kv0, kv1, kv2,
+    lat_h, rs_h, cnt_h, land_h, p0p, up, r0, q0, sres, coefs,
+    latp, rs6, cnt, land, weight, inv, kv0, kv1, kv2,
     psend, vrecv, precv, csend, crecv, redsend, redrecv,
-    plane_ss, plane_rs, col_ss, col_rs, red_ss, red_rs, in_sem, out_sem,
+    plane_ss, plane_rs, col_ss, col_rs, red_ss, red_rs, in_sem,
 ):
     days, lats, lons = rs6.shape
     last = days - 1
@@ -167,21 +167,32 @@
         wait_both(plane, rnd, 0, c)
 
         def complete(b, carry):
-            acc, total = carry
+            acc, totals = carry
             row = pl.multiple_of(c * CHUNK + b * BLOCK, BLOCK)
             rows = pl.ds(row, BLOCK)
+            wide = pl.ds(PAD + row, BLOCK)
             for d in range(days):
                 if d == 0 or d == last:
                     side = 0 if d == 0 else 1
                     tile = psend[rnd, side, rows] - vrecv[rnd, side, rows]
-                    kv[d, pl.ds(PAD + row, BLOCK)] = tile
+                    kv[d, wide] = tile
                 else:
-                    tile = kv[d, pl.ds(PAD + row, BLOCK)]
+                    tile = kv[d, wide]
                 acc = acc + gather(tile, d, b)
                 if rnd == 1:
-                    p = field[d, pl.ds(PAD + row, BLOCK)]
-                    total = total + fold(SCALE * tile * tile + weight[d, rows] * p * p)
-            return acc, total
+                    p = field[d, wide]
+                    totals = (totals[0] + fold(SCALE * tile * tile + weight[d, rows] * p * p),)
+                if rnd == 2:
+                    w, u = weight[d, rows], field[d, wide]
+                    z = p0p[d, wide] - u
+                    kz = kv1[d, wide] - tile
+                    skz, wz = SCALE * kz, w * z
+                    totals = (
+                        totals[0] + fold(skz * kz + wz * z),
+                        totals[1] + fold(skz * tile + wz * u),
+                        totals[2] + fold(SCALE * tile * tile + w * u * u),
+                    )
+            return acc, totals
 
         acc, total = unrolled(blocks, complete, (zeros, total))
         send_columns(rnd, 1, c, acc)
@@ -200,7 +211,7 @@
         field, kv = fields[rnd], kvs[rnd]
 
         def rest(b, carry):
-            acc, total = carry
+            acc, totals = carry
             row = pl.multiple_of(c * CHUNK + b * BLOCK, BLOCK)
             rows = pl.ds(row, BLOCK)
             wide = pl.ds(PAD + row, BLOCK)
@@ -215,18 +226,25 @@
                     value = residual * inv[d, rows]
                     r0[d, rows] = residual
                     p0p[d, wide] = value
-                    total = total + fold(residual * value)
                 else:
                     image = image + weight[d, rows] * field[d, wide]
                     if rnd == 1:
                         value = image * inv[d, rows]
                         q0[d, rows] = image
                         up[d, wide] = value
+                        p = field[d, wide]
+                        y, z = r0[d, rows] - image, p - value
+                        totals = (
+                            totals[0] + fold(y * p),
+                            totals[1] + fold(y * z),
+                            totals[2] + fold(y * value),
+                            totals[3] + fold(image * value),
+                        )
                     else:
                         sres[d, rows] = image
                 if rnd < ROUNDS - 1:
                     acc = acc + gather(value, d, b)
-            return acc, total
+            return acc, totals
 
         acc, total = unrolled(blocks, rest, (zeros, total))
         if rnd < ROUNDS - 1:
@@ -234,36 +252,34 @@
             send_columns(rnd + 1, 0, c, acc)
         return total
 
-    count = redsend.shape[2]
-
-    def peer_copy(which, stage, k):
+    def peer_copy(stage, k):
         peers = (lon_peer, day_peer)[stage]
         return pltpu.make_async_remote_copy(
-            src_ref=redsend.at[which, stage], dst_ref=redrecv.at[which, stage, k],
-            send_sem=red_ss.at[which, stage, k], recv_sem=red_rs.at[which, stage, k],
+            src_ref=redsend.at[stage], dst_ref=redrecv.at[stage, k],
+            send_sem=red_ss.at[stage, k], recv_sem=red_rs.at[stage, k],
             device_id=peers[k], device_id_type=MESH,
         )
 
-    def reduce_start(which, stage, values):
+    def reduce_start(stage, rows):
+        redsend[stage] = rows
+        for k in range(1, (n_lon, n_day)[stage]):
+            peer_copy(stage, k).start()
+
+    def reduce_wait(stage):
+        n = (n_lon, n_day)[stage]
+        total = redsend[stage]
+        for k in range(1, n):
+            peer_copy(stage, k).wait_recv()
+        for k in range(1, n):
+            total = total + redrecv[stage, k]
+        return total
+
+    def as_rows(values):
+        row = lax.broadcasted_iota(jnp.int32, (GROUP, lons), 0)
+        out = zeros
         for i, v in enumerate(values):
-            redsend[which, stage, i] = v
-        for k in range(1, (n_lon, n_day)[stage]):
-            peer_copy(which, stage, k).start()
-
-    def reduce_wait(which, stage, used):
-        n = (n_lon, n_day)[stage]
-        for k in range(1, n):
-            peer_copy(which, stage, k).wait_recv()
-        out = []
-        for i in range(used):
-            total = redsend[which, stage, i]
-            for k in range(1, n):
-                total = total + redrecv[which, stage, k, i]
-            out.append(total)
+            out = jnp.where(row == i, jnp.sum(v, axis=0, keepdims=True), out)
         return out
-
-    def scalar(x):
-        return jnp.sum(x)
 
     loads[0].wait()
     for ref in (latp, p0p, up, kv0, kv1, kv2):
@@ -303,76 +319,33 @@
 
     lax.fori_loop(0, lats // SMALL, prepare, 0)
 
-    m0 = m1 = zeros
+    sums = []
     for rnd in range(ROUNDS):
-        m1 = lax.fori_loop(0, chunks, functools.partial(first_k, rnd), m1)
-        if rnd == 1:
-            reduce_start(0, 0, [m0, m1])
+        start = ((), (zeros,), (zeros,) * 3)[rnd]
+        sums += lax.fori_loop(0, chunks, functools.partial(first_k, rnd), start)
         if rnd == 2:
-            s0, s1 = [scalar(v) for v in reduce_wait(0, 1, 2)]
-            rz0 = s0
-            a0 = jnp.full((SMALL, lons), s0) / jnp.full((SMALL, lons), s1)
-
-            def sums(b, carry):
-                rz, zq, zz = carry
-                row = pl.multiple_of(b * SMALL, SMALL)
-                rows = pl.ds(row, SMALL)
-                wide = pl.ds(PAD + row, SMALL)
-                for d in range(days):
-                    q = q0[d, rows]
-                    z = p0p[d, wide] - a0 * up[d, wide]
-                    kz = kv1[d, wide] - a0 * kv2[d, wide]
-                    rz = rz + fold((r0[d, rows] - a0 * q) * z)
-                    zq = zq + fold(z * q)
-                    zz = zz + fold(SCALE * kz * kz + weight[d, rows] * z * z)
-                return rz, zq, zz
-
-            reduce_start(1, 0, lax.fori_loop(0, lats // SMALL, sums, (zeros, zeros, zeros)))
+            reduce_start(0, as_rows(sums))
         turn = functools.partial(second_k, rnd)
-        if rnd == 0:
-            m0 = lax.fori_loop(0, chunks, turn, m0)
+        if rnd < 2:
+            sums += lax.fori_loop(0, chunks, turn, ((), (zeros,) * 4)[rnd])
         else:
-            split = chunks - 2
-            lax.fori_loop(0, split, turn, zeros)
-            reduce_start(rnd - 1, 1, reduce_wait(rnd - 1, 0, (2, 3)[rnd - 1]))
-            lax.fori_loop(split, chunks, turn, zeros)
-
-    t0, t1, t2 = [scalar(v) for v in reduce_wait(1, 1, 3)]
-    wide_of = lambda v: jnp.full((SMALL, lons), v)
-    rz1, zq, zz = wide_of(t0), wide_of(t1), wide_of(t2)
-    beta = rz1 / wide_of(rz0)
-    a1 = rz1 / (zz + 2.0 * beta * zq + beta * beta * wide_of(s1))
-    coef_p = a0 + a1 * (1.0 + beta)
-    coef_u = a0 * a1
-
-    def out_copies(c):
-        rows = pl.ds(c * CHUNK, CHUNK)
-        return (
-            pltpu.make_async_copy(q0.at[:, rows], step_h.at[:, rows], out_sem.at[0, c]),
-            pltpu.make_async_copy(sres.at[:, rows], res_h.at[:, rows], out_sem.at[1, c]),
-        )
-
-    def finish(c, carry):
-        def one(b, carry):
-            row = pl.multiple_of(c * CHUNK + b * SMALL, SMALL)
-            rows = pl.ds(row, SMALL)
-            wide = pl.ds(PAD + row, SMALL)
-            for d in range(days):
-                q = q0[d, rows]
-                sres[d, rows] = r0[d, rows] - coef_p * q + coef_u * sres[d, rows]
-                q0[d, rows] = coef_p * p0p[d, wide] - coef_u * up[d, wide]
-            return carry
-
-        lax.fori_loop(0, CHUNK // SMALL, one, 0)
-        for copy in out_copies(c):
-            copy.start()
-        return carry
-
-    lax.fori_loop(0, chunks, finish, 0)
+            lax.fori_loop(0, chunks - 1, turn, ())
+            reduce_start(1, reduce_wait(0))
+            turn(chunks - 1, ())
+
+    all_sums = jnp.sum(reduce_wait(1), axis=1, keepdims=True)
+    m1, n1, n2, n3, m2, zz, zu, uu = [jnp.broadcast_to(all_sums[i:i + 1], (1, lons)) for i in range(GROUP)]
+    extra = n1 / m1
+    a0 = 1.0 + extra
+    rz1 = n2 - 2.0 * extra * n3 + extra * extra * m2
+    beta = rz1 / (m1 + n1)
+    zq = n3 - extra * m2
+    zhz = zz - 2.0 * extra * zu + extra * extra * uu
+    a1 = rz1 / (zhz + 2.0 * beta * zq + beta * beta * m1)
+    coefs[0:1] = a0 + a1 * (1.0 + beta)
+    coefs[1:2] = a0 * a1
 
     def drain(c, carry):
-        for copy in out_copies(c):
-            copy.wait()
         for rnd in range(ROUNDS):
             for kind in range(2):
                 for side in range(2):
@@ -381,10 +354,9 @@
         return carry
 
     lax.fori_loop(0, chunks, drain, 0)
-    for which in range(2):
-        for stage in range(2):
-            for k in range(1, (n_lon, n_day)[stage]):
-                peer_copy(which, stage, k).wait_send()
+    for stage in range(2):
+        for k in range(1, (n_lon, n_day)[stage]):
+            peer_copy(stage, k).wait_send()
 
 
 def solution(mesh):
@@ -400,27 +372,33 @@
         padded = (days, lats + 2 * PAD, lons)
         vmem = pltpu.VMEM
         dma = pltpu.SemaphoreType.DMA
-        return pl.pallas_call(
+        p0, u, r0, q0, s, coefs = pl.pallas_call(
             functools.partial(kernel, names, n_day, n_lon),
-            out_shape=[jax.ShapeDtypeStruct(whole, f32)] * 2,
+            out_shape=[
+                vmem(padded, f32), vmem(padded, f32), vmem(whole, f32), vmem(whole, f32), vmem(whole, f32),
+                vmem((2, lons), f32),
+            ],
             in_specs=[pl.BlockSpec(memory_space=pl.ANY)] * 4,
-            out_specs=[pl.BlockSpec(memory_space=pl.ANY)] * 2,
+            out_specs=[pl.BlockSpec(memory_space=pltpu.VMEM)] * 6,
             scratch_shapes=[
                 vmem(padded, f32), vmem(whole, f32), vmem(whole, jnp.int32), vmem(whole, jnp.int32),
-                vmem(whole, f32), vmem(whole, f32), vmem(padded, f32), vmem(padded, f32),
-                vmem(whole, f32), vmem(whole, f32), vmem(whole, f32),
+                vmem(whole, f32), vmem(whole, f32),
                 vmem(padded, f32), vmem(padded, f32), vmem(padded, f32),
                 vmem((ROUNDS, 2, lats, lons), f32), vmem((ROUNDS, 2, lats, lons), f32),
                 vmem((ROUNDS, 2, lats, lons), f32),
                 vmem((ROUNDS, 2, chunks, GROUP, lons), f32), vmem((ROUNDS, 2, chunks, 2, GROUP, lons), f32),
-                vmem((2, 2, 3, GROUP, lons), f32), vmem((2, 2, n_lon, 3, GROUP, lons), f32),
+                vmem((2, GROUP, lons), f32), vmem((2, n_lon, GROUP, lons), f32),
                 dma((ROUNDS, 2, chunks, 2)), dma((ROUNDS, 2, chunks, 2)),
                 dma((ROUNDS, 2, chunks, 2)), dma((ROUNDS, 2, chunks, 2)),
-                dma((2, 2, n_lon)), dma((2, 2, n_lon)), dma((4,)), dma((2, chunks)),
+                dma((2, n_lon)), dma((2, n_lon)), dma((4,)),
             ],
             compiler_params=pltpu.CompilerParams(
-                collective_id=0, has_side_effects=True, vmem_limit_bytes=60 << 20
+                collective_id=0, has_side_effects=True, vmem_limit_bytes=44 << 20
             ),
         )(latent, range_sq, counts, land)
+        body = slice(PAD, PAD + lats)
+        step = coefs[0] * p0[:, body] - coefs[1] * u[:, body]
+        residual = r0 - coefs[0] * q0 + coefs[1] * s
+        return step, residual
 
     return jax.shard_map(per_device, mesh=mesh, in_specs=(spec,) * 4, out_specs=(spec, spec), check_vma=False)

time: 62.7 us -> 55.9 us (0.89)
  Pallas kernels: 57.4 us -> 52.6 us
  local copies, waits for them, and re-layouts: 4.52 us -> 0.01 us
  other arithmetic: 0 us -> 2.51 us
    pallas_call x1, Pallas kernels: 57.4 us -> 52.6 us  [per_device(): pl.pallas_call(functools.partial(kernel, names, n_day, n_lon), out_shape=...]
    unnamed x4 -> x0, local copies, waits for them, and re-layouts: 4.52 us -> none
    add x0 -> x1, other arithmetic: none -> 2.51 us  [per_device(): residual = r0 - coefs[0] * q0 + coefs[1] * s]
where the time goes in v3:
time: 55.9 us; the launch traced here: 55.8 us
  Pallas kernels  52.6 us (94%)
  other arithmetic  2.51 us (4%)
  between operations  0.65 us (1%)
    pallas_call x1, Pallas kernels, per_device(): pl.pallas_call(functools.partial(kernel, names, n_day, n_lon), out_shape=...  52.6 us
    add x1, other arithmetic, per_device(): residual = r0 - coefs[0] * q0 + coefs[1] * s  2.51 us

profile of v3, /device:TPU:1, one launch (start us, length us, event | category | flops | bytes accessed | tf_op | source)
XLA Modules:
  0.0 55.8 jit_solution(17015884323748841962)
XLA Ops:
  0.6 52.6 %shard_map.59 = (f32[4,1040,128]{2,1,0:T(8,128)S(1)}, f32[4,1040,128]{2,1,0:T(8,128)S(1)}, f32[4,1024,128]{2,1,0:T(8,128)S(1)}, f32[4,1024,128]{2,1,0:T(8,128)S(...) custom-call(f32[4,1024,128]{2,1,0:T(8,128)} %lat_h.1, f32[4,1024,128]{2,1,0:T(8,128)} %rs_h.1, ...), custom_call_target="tpu_custom_call" | custom-call | tf_op jit(solution)/shard_map/pallas_call | solution.py:375
  53.3 2.5 %multiply_add_fusion = (f32[4,1024,128]{2,1,0:T(8,128)}, f32[4,1024,128]{2,1,0:T(8,128)}) fusion(f32[4,1024,128]{2,1,0:T(8,128)S(1)} %get-tuple-element.13, f32[4,1024,128]{2,1,0:T(8,128)S(1)} %get-tuple-element.11, f32[4,1024,128]{2,1,0:T(8,128)S(1)} %get-tuple-element.12, f32[128]{0:T(128)S(1)} %get-tuple-element.17, f32[128]{0:T(128)S(1)} %get-tuple-element.16, ...), kind=kLoop, calls=%fused_computation | loop fusion | flops 3670016 | bytes 14681088 | tf_op jit(solution)/shard_map/add | solution.py:401
  (1 shorter events, 0.0 us)

commit v4 on v3

--- a/solution.py
+++ b/solution.py
@@ -14,6 +14,7 @@
 CHUNK = 128
 BLOCK = 128
 SMALL = 64
+HELD = 3
 MESH = pl.DeviceIdType.MESH
 
 
@@ -49,9 +50,6 @@
         pltpu.make_async_copy(land_h, land, in_sem.at[2]),
         pltpu.make_async_copy(cnt_h, cnt, in_sem.at[3]),
     ]
-    for copy in loads:
-        copy.start()
-
     barrier = pltpu.get_barrier_semaphore()
     for peer in day_peer[1:] + lon_peer[1:]:
         pl.semaphore_signal(barrier, inc=1, device_id=peer, device_id_type=MESH)
@@ -61,27 +59,27 @@
     kvs = (kv0, kv1, kv2)
     edges = (0, last)
 
-    def plane(rnd, kind, c, side):
-        rows = pl.ds(c * CHUNK, CHUNK)
+    def plane(rnd, kind, c, side, size=CHUNK):
+        rows = pl.ds(c * CHUNK, size)
         if kind == 0:
             if rnd == 0:
                 src = lat_h.at[edges[side], rows]
             else:
-                src = fields[rnd].at[edges[side], pl.ds(PAD + c * CHUNK, CHUNK)]
+                src = fields[rnd].at[edges[side], pl.ds(PAD + c * CHUNK, size)]
             dst = vrecv.at[rnd, 1 - side, rows]
         else:
             src = psend.at[rnd, side, rows]
             dst = precv.at[rnd, 1 - side, rows]
         return pltpu.make_async_remote_copy(
             src_ref=src, dst_ref=dst,
-            send_sem=plane_ss.at[rnd, kind, c, side], recv_sem=plane_rs.at[rnd, kind, c, 1 - side],
+            send_sem=plane_ss.at[rnd, kind, side], recv_sem=plane_rs.at[rnd, kind, c, 1 - side],
             device_id=sides[side], device_id_type=MESH,
         )
 
     def column(rnd, kind, c, side):
         return pltpu.make_async_remote_copy(
-            src_ref=csend.at[rnd, kind, c], dst_ref=crecv.at[rnd, kind, c, 1 - side],
-            send_sem=col_ss.at[rnd, kind, c, side], recv_sem=col_rs.at[rnd, kind, c, 1 - side],
+            src_ref=csend.at[rnd, kind, c], dst_ref=crecv.at[rnd, kind, 1 - side, c],
+            send_sem=col_ss.at[rnd, kind, side], recv_sem=col_rs.at[rnd, kind, c, 1 - side],
             device_id=beside[side], device_id_type=MESH,
         )
 
@@ -90,6 +88,13 @@
             carry = body(i, carry)
         return carry
 
+    def all_columns(rnd, kind, side):
+        return pltpu.make_async_remote_copy(
+            src_ref=csend.at[rnd, kind], dst_ref=crecv.at[rnd, kind, 1 - side],
+            send_sem=col_ss.at[rnd, kind, side], recv_sem=col_rs.at[rnd, kind, 0, 1 - side],
+            device_id=beside[side], device_id_type=MESH,
+        )
+
     def start_both(copy, rnd, kind, c):
         copy(rnd, kind, c, 0).start()
         copy(rnd, kind, c, 1).start()
@@ -103,6 +108,8 @@
         return carry
 
     lax.fori_loop(0, chunks, first_planes, 0)
+    for copy in loads:
+        copy.start()
 
     lane = lax.broadcasted_iota(jnp.int32, (GROUP, lons), 1)
     pair = ((lane + 1) & (lons - 1)) >> 1
@@ -120,8 +127,8 @@
         return acc
 
     def outer_columns(rnd, kind, c):
-        low = crecv[rnd, kind, c, 0]
-        high = crecv[rnd, kind, c, 1]
+        low = crecv[rnd, kind, 0, c]
+        high = crecv[rnd, kind, 1, c]
         return jnp.where(even, pltpu.roll(low, 1, 1), pltpu.roll(high, lons - 1, 1))
 
     def along_lon(x, cols, d, b):
@@ -147,7 +154,7 @@
         csend[rnd, kind, c] = acc
         start_both(column, rnd, kind, c)
 
-    def first_k(rnd, c, total):
+    def first_k(rnd, send, c, total):
         wait_both(column, rnd, 0, c)
         cols = outer_columns(rnd, 0, c)
         field, kv = fields[rnd], kvs[rnd]
@@ -163,7 +170,8 @@
             return carry
 
         unrolled(blocks, partial, 0)
-        start_both(plane, rnd, 1, c)
+        if send:
+            start_both(plane, rnd, 1, c)
         wait_both(plane, rnd, 0, c)
 
         def complete(b, carry):
@@ -253,7 +261,7 @@
         return total
 
     def peer_copy(stage, k):
-        peers = (lon_peer, day_peer)[stage]
+        peers = (day_peer, lon_peer)[stage]
         return pltpu.make_async_remote_copy(
             src_ref=redsend.at[stage], dst_ref=redrecv.at[stage, k],
             send_sem=red_ss.at[stage, k], recv_sem=red_rs.at[stage, k],
@@ -262,11 +270,11 @@
 
     def reduce_start(stage, rows):
         redsend[stage] = rows
-        for k in range(1, (n_lon, n_day)[stage]):
+        for k in range(1, (n_day, n_lon)[stage]):
             peer_copy(stage, k).start()
 
     def reduce_wait(stage):
-        n = (n_lon, n_day)[stage]
+        n = (n_day, n_lon)[stage]
         total = redsend[stage]
         for k in range(1, n):
             peer_copy(stage, k).wait_recv()
@@ -320,18 +328,27 @@
     lax.fori_loop(0, lats // SMALL, prepare, 0)
 
     sums = []
+    for rnd in range(ROUNDS - 1):
+        sums += lax.fori_loop(0, chunks, functools.partial(first_k, rnd, True), ((), (zeros,))[rnd])
+        sums += lax.fori_loop(0, chunks, functools.partial(second_k, rnd), ((), (zeros,) * 4)[rnd])
+
+    rnd = ROUNDS - 1
+    total = lax.fori_loop(0, chunks - HELD, functools.partial(first_k, rnd, True), (zeros,) * 3)
+    sums += lax.fori_loop(chunks - HELD, chunks, functools.partial(first_k, rnd, False), total)
+    reduce_start(0, as_rows(sums))
+    for c in range(chunks - HELD, chunks):
+        start_both(plane, rnd, 1, c)
+    lax.fori_loop(0, chunks - HELD, functools.partial(second_k, rnd), ())
+    reduce_start(1, reduce_wait(0))
+    lax.fori_loop(chunks - HELD, chunks, functools.partial(second_k, rnd), ())
+
     for rnd in range(ROUNDS):
-        start = ((), (zeros,), (zeros,) * 3)[rnd]
-        sums += lax.fori_loop(0, chunks, functools.partial(first_k, rnd), start)
-        if rnd == 2:
-            reduce_start(0, as_rows(sums))
-        turn = functools.partial(second_k, rnd)
-        if rnd < 2:
-            sums += lax.fori_loop(0, chunks, turn, ((), (zeros,) * 4)[rnd])
-        else:
-            lax.fori_loop(0, chunks - 1, turn, ())
-            reduce_start(1, reduce_wait(0))
-            turn(chunks - 1, ())
+        for kind in range(2):
+            for side in range(2):
+                plane(rnd, kind, 0, side, lats).wait_send()
+                all_columns(rnd, kind, side).wait_send()
+    for k in range(1, n_day):
+        peer_copy(0, k).wait_send()
 
     all_sums = jnp.sum(reduce_wait(1), axis=1, keepdims=True)
     m1, n1, n2, n3, m2, zz, zu, uu = [jnp.broadcast_to(all_sums[i:i + 1], (1, lons)) for i in range(GROUP)]
@@ -345,18 +362,8 @@
     coefs[0:1] = a0 + a1 * (1.0 + beta)
     coefs[1:2] = a0 * a1
 
-    def drain(c, carry):
-        for rnd in range(ROUNDS):
-            for kind in range(2):
-                for side in range(2):
-                    plane(rnd, kind, c, side).wait_send()
-                    column(rnd, kind, c, side).wait_send()
-        return carry
-
-    lax.fori_loop(0, chunks, drain, 0)
-    for stage in range(2):
-        for k in range(1, (n_lon, n_day)[stage]):
-            peer_copy(stage, k).wait_send()
+    for k in range(1, n_lon):
+        peer_copy(1, k).wait_send()
 
 
 def solution(mesh):
@@ -386,10 +393,10 @@
                 vmem(padded, f32), vmem(padded, f32), vmem(padded, f32),
                 vmem((ROUNDS, 2, lats, lons), f32), vmem((ROUNDS, 2, lats, lons), f32),
                 vmem((ROUNDS, 2, lats, lons), f32),
-                vmem((ROUNDS, 2, chunks, GROUP, lons), f32), vmem((ROUNDS, 2, chunks, 2, GROUP, lons), f32),
+                vmem((ROUNDS, 2, chunks, GROUP, lons), f32), vmem((ROUNDS, 2, 2, chunks, GROUP, lons), f32),
                 vmem((2, GROUP, lons), f32), vmem((2, n_lon, GROUP, lons), f32),
-                dma((ROUNDS, 2, chunks, 2)), dma((ROUNDS, 2, chunks, 2)),
-                dma((ROUNDS, 2, chunks, 2)), dma((ROUNDS, 2, chunks, 2)),
+                dma((ROUNDS, 2, 2)), dma((ROUNDS, 2, chunks, 2)),
+                dma((ROUNDS, 2, 2)), dma((ROUNDS, 2, chunks, 2)),
                 dma((2, n_lon)), dma((2, n_lon)), dma((4,)),
             ],
             compiler_params=pltpu.CompilerParams(

time: 55.9 us -> 53.6 us (0.959)
  Pallas kernels: 52.6 us -> 50.3 us
    pallas_call x1, Pallas kernels: 52.6 us -> 50.3 us  [per_device(): pl.pallas_call(functools.partial(kernel, names, n_day, n_lon), out_shape=...]
where the time goes in v4:
time: 53.6 us; the launch traced here: 53.5 us
  Pallas kernels  50.3 us (94%)
  other arithmetic  2.51 us (5%)
  between operations  0.65 us (1%)
    pallas_call x1, Pallas kernels, per_device(): pl.pallas_call(functools.partial(kernel, names, n_day, n_lon), out_shape=...  50.3 us
    add x1, other arithmetic, per_device(): residual = r0 - coefs[0] * q0 + coefs[1] * s  2.51 us

profile of v4, /device:TPU:1, one launch (start us, length us, event | category | flops | bytes accessed | tf_op | source)
XLA Modules:
  0.0 53.5 jit_solution(13758161329460636748)
XLA Ops:
  0.6 50.3 %shard_map.59 = (f32[4,1040,128]{2,1,0:T(8,128)S(1)}, f32[4,1040,128]{2,1,0:T(8,128)S(1)}, f32[4,1024,128]{2,1,0:T(8,128)S(1)}, f32[4,1024,128]{2,1,0:T(8,128)S(...) custom-call(f32[4,1024,128]{2,1,0:T(8,128)} %lat_h.1, f32[4,1024,128]{2,1,0:T(8,128)} %rs_h.1, ...), custom_call_target="tpu_custom_call" | custom-call | tf_op jit(solution)/shard_map/pallas_call | solution.py:382
  51.0 2.5 %multiply_add_fusion = (f32[4,1024,128]{2,1,0:T(8,128)}, f32[4,1024,128]{2,1,0:T(8,128)}) fusion(f32[4,1024,128]{2,1,0:T(8,128)S(1)} %get-tuple-element.13, f32[4,1024,128]{2,1,0:T(8,128)S(1)} %get-tuple-element.11, f32[4,1024,128]{2,1,0:T(8,128)S(1)} %get-tuple-element.12, f32[128]{0:T(128)S(1)} %get-tuple-element.17, f32[128]{0:T(128)S(1)} %get-tuple-element.16, ...), kind=kLoop, calls=%fused_computation | loop fusion | flops 3670016 | bytes 14681088 | tf_op jit(solution)/shard_map/add | solution.py:408
  (1 shorter events, 0.0 us)

commit v5 on v4

--- a/solution.py
+++ b/solution.py
@@ -12,9 +12,11 @@
 PAD = 8
 GROUP = 8
 CHUNK = 128
+MERGE = ((2, 2), (2, 2), (1, 2))
+TURN = 2
 BLOCK = 128
 SMALL = 64
-HELD = 3
+HELD = 2
 MESH = pl.DeviceIdType.MESH
 
 
@@ -50,6 +52,7 @@
         pltpu.make_async_copy(land_h, land, in_sem.at[2]),
         pltpu.make_async_copy(cnt_h, cnt, in_sem.at[3]),
     ]
+    loads[0].start()
     barrier = pltpu.get_barrier_semaphore()
     for peer in day_peer[1:] + lon_peer[1:]:
         pl.semaphore_signal(barrier, inc=1, device_id=peer, device_id_type=MESH)
@@ -59,7 +62,9 @@
     kvs = (kv0, kv1, kv2)
     edges = (0, last)
 
-    def plane(rnd, kind, c, side, size=CHUNK):
+    def plane(rnd, kind, c, side, size=None):
+        if size is None:
+            size = CHUNK * MERGE[rnd][kind]
         rows = pl.ds(c * CHUNK, size)
         if kind == 0:
             if rnd == 0:
@@ -103,12 +108,9 @@
         copy(rnd, kind, c, 0).wait_recv()
         copy(rnd, kind, c, 1).wait_recv()
 
-    def first_planes(c, carry):
+    for c in range(0, chunks, MERGE[0][0]):
         start_both(plane, 0, 0, c)
-        return carry
-
-    lax.fori_loop(0, chunks, first_planes, 0)
-    for copy in loads:
+    for copy in loads[1:]:
         copy.start()
 
     lane = lax.broadcasted_iota(jnp.int32, (GROUP, lons), 1)
@@ -154,7 +156,7 @@
         csend[rnd, kind, c] = acc
         start_both(column, rnd, kind, c)
 
-    def first_k(rnd, send, c, total):
+    def first_part(rnd, c):
         wait_both(column, rnd, 0, c)
         cols = outer_columns(rnd, 0, c)
         field, kv = fields[rnd], kvs[rnd]
@@ -170,9 +172,11 @@
             return carry
 
         unrolled(blocks, partial, 0)
-        if send:
-            start_both(plane, rnd, 1, c)
-        wait_both(plane, rnd, 0, c)
+
+    def first_rest(rnd, c, total):
+        if MERGE[rnd][0] == 1:
+            wait_both(plane, rnd, 0, c)
+        field, kv = fields[rnd], kvs[rnd]
 
         def complete(b, carry):
             acc, totals = carry
@@ -206,15 +210,28 @@
         send_columns(rnd, 1, c, acc)
         return total
 
+    def first_k(rnd, send, m, total):
+        c = m * TURN
+
+        def part(h, carry):
+            first_part(rnd, c + h)
+            return carry
+
+        lax.fori_loop(0, TURN, part, 0)
+        if send:
+            start_both(plane, rnd, 1, c)
+        if MERGE[rnd][0] == TURN:
+            wait_both(plane, rnd, 0, c)
+        return lax.fori_loop(0, TURN, lambda h, t: first_rest(rnd, c + h, t), total)
+
     def fold(x):
         while x.shape[0] > GROUP:
             half = x.shape[0] // 2
             x = x[:half] + x[half:]
         return x
 
-    def second_k(rnd, c, total):
+    def second_part(rnd, c, total):
         wait_both(column, rnd, 1, c)
-        wait_both(plane, rnd, 1, c)
         cols = outer_columns(rnd, 1, c)
         field, kv = fields[rnd], kvs[rnd]
 
@@ -256,8 +273,17 @@
 
         acc, total = unrolled(blocks, rest, (zeros, total))
         if rnd < ROUNDS - 1:
+            if MERGE[rnd + 1][0] == 1:
+                start_both(plane, rnd + 1, 0, c)
+            send_columns(rnd + 1, 0, c, acc)
+        return total
+
+    def second_k(rnd, m, total):
+        c = m * TURN
+        wait_both(plane, rnd, 1, c)
+        total = lax.fori_loop(0, TURN, lambda h, t: second_part(rnd, c + h, t), total)
+        if rnd < ROUNDS - 1 and MERGE[rnd + 1][0] == TURN:
             start_both(plane, rnd + 1, 0, c)
-            send_columns(rnd + 1, 0, c, acc)
         return total
 
     def peer_copy(stage, k):
@@ -327,20 +353,21 @@
 
     lax.fori_loop(0, lats // SMALL, prepare, 0)
 
+    turns = chunks // TURN
     sums = []
     for rnd in range(ROUNDS - 1):
-        sums += lax.fori_loop(0, chunks, functools.partial(first_k, rnd, True), ((), (zeros,))[rnd])
-        sums += lax.fori_loop(0, chunks, functools.partial(second_k, rnd), ((), (zeros,) * 4)[rnd])
+        sums += lax.fori_loop(0, turns, functools.partial(first_k, rnd, True), ((), (zeros,))[rnd])
+        sums += lax.fori_loop(0, turns, functools.partial(second_k, rnd), ((), (zeros,) * 4)[rnd])
 
     rnd = ROUNDS - 1
-    total = lax.fori_loop(0, chunks - HELD, functools.partial(first_k, rnd, True), (zeros,) * 3)
-    sums += lax.fori_loop(chunks - HELD, chunks, functools.partial(first_k, rnd, False), total)
+    total = lax.fori_loop(0, turns - HELD, functools.partial(first_k, rnd, True), (zeros,) * 3)
+    sums += lax.fori_loop(turns - HELD, turns, functools.partial(first_k, rnd, False), total)
     reduce_start(0, as_rows(sums))
-    for c in range(chunks - HELD, chunks):
-        start_both(plane, rnd, 1, c)
-    lax.fori_loop(0, chunks - HELD, functools.partial(second_k, rnd), ())
+    for c in range(turns - HELD, turns):
+        start_both(plane, rnd, 1, c * TURN)
+    lax.fori_loop(0, turns - HELD, functools.partial(second_k, rnd), ())
     reduce_start(1, reduce_wait(0))
-    lax.fori_loop(chunks - HELD, chunks, functools.partial(second_k, rnd), ())
+    lax.fori_loop(turns - HELD, turns, functools.partial(second_k, rnd), ())
 
     for rnd in range(ROUNDS):
         for kind in range(2):

time: 53.6 us -> 52.6 us (0.981)
  Pallas kernels: 50.3 us -> 49.3 us
    pallas_call x1, Pallas kernels: 50.3 us -> 49.3 us  [per_device(): pl.pallas_call(functools.partial(kernel, names, n_day, n_lon), out_shape=...]
where the time goes in v5:
time: 52.6 us; the launch traced here: 52.5 us
  Pallas kernels  49.3 us (94%)
  other arithmetic  2.51 us (5%)
  between operations  0.65 us (1%)
    pallas_call x1, Pallas kernels, per_device(): pl.pallas_call(functools.partial(kernel, names, n_day, n_lon), out_shape=...  49.3 us
    add x1, other arithmetic, per_device(): residual = r0 - coefs[0] * q0 + coefs[1] * s  2.51 us

profile of v5, /device:TPU:1, one launch (start us, length us, event | category | flops | bytes accessed | tf_op | source)
XLA Modules:
  0.0 52.5 jit_solution(12671378786734278520)
XLA Ops:
  0.6 49.3 %shard_map.59 = (f32[4,1040,128]{2,1,0:T(8,128)S(1)}, f32[4,1040,128]{2,1,0:T(8,128)S(1)}, f32[4,1024,128]{2,1,0:T(8,128)S(1)}, f32[4,1024,128]{2,1,0:T(8,128)S(...) custom-call(f32[4,1024,128]{2,1,0:T(8,128)} %lat_h.1, f32[4,1024,128]{2,1,0:T(8,128)} %rs_h.1, ...), custom_call_target="tpu_custom_call" | custom-call | tf_op jit(solution)/shard_map/pallas_call | solution.py:409
  50.0 2.5 %multiply_add_fusion = (f32[4,1024,128]{2,1,0:T(8,128)}, f32[4,1024,128]{2,1,0:T(8,128)}) fusion(f32[4,1024,128]{2,1,0:T(8,128)S(1)} %get-tuple-element.13, f32[4,1024,128]{2,1,0:T(8,128)S(1)} %get-tuple-element.11, f32[4,1024,128]{2,1,0:T(8,128)S(1)} %get-tuple-element.12, f32[128]{0:T(128)S(1)} %get-tuple-element.17, f32[128]{0:T(128)S(1)} %get-tuple-element.16, ...), kind=kLoop, calls=%fused_computation | loop fusion | flops 3670016 | bytes 14681088 | tf_op jit(solution)/shard_map/add | solution.py:435
  (1 shorter events, 0.0 us)

commit v6 on v5

--- a/solution.py
+++ b/solution.py
@@ -62,9 +62,12 @@
     kvs = (kv0, kv1, kv2)
     edges = (0, last)
 
-    def plane(rnd, kind, c, side, size=None):
-        if size is None:
-            size = CHUNK * MERGE[rnd][kind]
+    def slot(rnd, c, merge):
+        at = c // merge if isinstance(c, int) else lax.div(c, merge)
+        return at + (chunks if rnd == 1 else 0)
+
+    def plane(rnd, kind, c, side):
+        size = CHUNK * MERGE[rnd][kind]
         rows = pl.ds(c * CHUNK, size)
         if kind == 0:
             if rnd == 0:
@@ -77,14 +80,15 @@
             dst = precv.at[rnd, 1 - side, rows]
         return pltpu.make_async_remote_copy(
             src_ref=src, dst_ref=dst,
-            send_sem=plane_ss.at[rnd, kind, side], recv_sem=plane_rs.at[rnd, kind, c, 1 - side],
+            send_sem=plane_ss.at[kind], recv_sem=plane_rs.at[kind, slot(rnd, c, MERGE[rnd][kind]), 1 - side],
             device_id=sides[side], device_id_type=MESH,
         )
 
-    def column(rnd, kind, c, side):
+    def column(rnd, kind, m, side):
+        tiles = pl.ds(0, chunks) if rnd == kind == 0 else pl.ds(m * TURN, TURN)
         return pltpu.make_async_remote_copy(
-            src_ref=csend.at[rnd, kind, c], dst_ref=crecv.at[rnd, kind, 1 - side, c],
-            send_sem=col_ss.at[rnd, kind, side], recv_sem=col_rs.at[rnd, kind, c, 1 - side],
+            src_ref=csend.at[rnd, kind, tiles], dst_ref=crecv.at[1 - side, rnd, kind, tiles],
+            send_sem=col_ss.at[side], recv_sem=col_rs.at[kind, m + (chunks // TURN if rnd == 1 else 0), 1 - side],
             device_id=beside[side], device_id_type=MESH,
         )
 
@@ -92,13 +96,6 @@
         for i in range(n):
             carry = body(i, carry)
         return carry
-
-    def all_columns(rnd, kind, side):
-        return pltpu.make_async_remote_copy(
-            src_ref=csend.at[rnd, kind], dst_ref=crecv.at[rnd, kind, 1 - side],
-            send_sem=col_ss.at[rnd, kind, side], recv_sem=col_rs.at[rnd, kind, 0, 1 - side],
-            device_id=beside[side], device_id_type=MESH,
-        )
 
     def start_both(copy, rnd, kind, c):
         copy(rnd, kind, c, 0).start()
@@ -129,8 +126,8 @@
         return acc
 
     def outer_columns(rnd, kind, c):
-        low = crecv[rnd, kind, 0, c]
-        high = crecv[rnd, kind, 1, c]
+        low = crecv[0, rnd, kind, c]
+        high = crecv[1, rnd, kind, c]
         return jnp.where(even, pltpu.roll(low, 1, 1), pltpu.roll(high, lons - 1, 1))
 
     def along_lon(x, cols, d, b):
@@ -152,12 +149,7 @@
             out.append(rs6[d, pl.ds(row, BLOCK)] * x[d] - near)
         return out
 
-    def send_columns(rnd, kind, c, acc):
-        csend[rnd, kind, c] = acc
-        start_both(column, rnd, kind, c)
-
     def first_part(rnd, c):
-        wait_both(column, rnd, 0, c)
         cols = outer_columns(rnd, 0, c)
         field, kv = fields[rnd], kvs[rnd]
 
@@ -207,11 +199,13 @@
             return acc, totals
 
         acc, total = unrolled(blocks, complete, (zeros, total))
-        send_columns(rnd, 1, c, acc)
+        csend[rnd, 1, c] = acc
         return total
 
     def first_k(rnd, send, m, total):
         c = m * TURN
+        if rnd > 0:
+            wait_both(column, rnd, 0, m)
 
         def part(h, carry):
             first_part(rnd, c + h)
@@ -222,7 +216,9 @@
             start_both(plane, rnd, 1, c)
         if MERGE[rnd][0] == TURN:
             wait_both(plane, rnd, 0, c)
-        return lax.fori_loop(0, TURN, lambda h, t: first_rest(rnd, c + h, t), total)
+        total = lax.fori_loop(0, TURN, lambda h, t: first_rest(rnd, c + h, t), total)
+        start_both(column, rnd, 1, m)
+        return total
 
     def fold(x):
         while x.shape[0] > GROUP:
@@ -231,7 +227,6 @@
         return x
 
     def second_part(rnd, c, total):
-        wait_both(column, rnd, 1, c)
         cols = outer_columns(rnd, 1, c)
         field, kv = fields[rnd], kvs[rnd]
 
@@ -275,23 +270,33 @@
         if rnd < ROUNDS - 1:
             if MERGE[rnd + 1][0] == 1:
                 start_both(plane, rnd + 1, 0, c)
-            send_columns(rnd + 1, 0, c, acc)
+            csend[rnd + 1, 0, c] = acc
         return total
 
     def second_k(rnd, m, total):
         c = m * TURN
+        wait_both(column, rnd, 1, m)
         wait_both(plane, rnd, 1, c)
         total = lax.fori_loop(0, TURN, lambda h, t: second_part(rnd, c + h, t), total)
         if rnd < ROUNDS - 1 and MERGE[rnd + 1][0] == TURN:
             start_both(plane, rnd + 1, 0, c)
+        if rnd < ROUNDS - 1:
+            start_both(column, rnd + 1, 0, m)
         return total
 
     def peer_copy(stage, k):
         peers = (day_peer, lon_peer)[stage]
         return pltpu.make_async_remote_copy(
             src_ref=redsend.at[stage], dst_ref=redrecv.at[stage, k],
-            send_sem=red_ss.at[stage, k], recv_sem=red_rs.at[stage, k],
+            send_sem=red_ss.at[stage], recv_sem=red_rs.at[stage],
             device_id=peers[k], device_id_type=MESH,
+        )
+
+    def all_peers(stage):
+        others = redrecv.at[stage, pl.ds(1, (n_day, n_lon)[stage] - 1)]
+        return pltpu.make_async_remote_copy(
+            src_ref=others, dst_ref=others, send_sem=red_ss.at[stage], recv_sem=red_rs.at[stage],
+            device_id=(day_peer, lon_peer)[stage][1], device_id_type=MESH,
         )
 
     def reduce_start(stage, rows):
@@ -302,8 +307,7 @@
     def reduce_wait(stage):
         n = (n_day, n_lon)[stage]
         total = redsend[stage]
-        for k in range(1, n):
-            peer_copy(stage, k).wait_recv()
+        all_peers(stage).wait_recv()
         for k in range(1, n):
             total = total + redrecv[stage, k]
         return total
@@ -328,10 +332,11 @@
                 acc = acc + gather(latp[d, pl.ds(PAD + row, BLOCK)], d, b)
             return acc
 
-        send_columns(0, 0, c, unrolled(blocks, step, zeros))
+        csend[0, 0, c] = unrolled(blocks, step, zeros)
         return carry
 
     lax.fori_loop(0, chunks, first_columns, 0)
+    start_both(column, 0, 0, 0)
 
     for copy in loads[1:]:
         copy.wait()
@@ -355,6 +360,7 @@
 
     turns = chunks // TURN
     sums = []
+    wait_both(column, 0, 0, 0)
     for rnd in range(ROUNDS - 1):
         sums += lax.fori_loop(0, turns, functools.partial(first_k, rnd, True), ((), (zeros,))[rnd])
         sums += lax.fori_loop(0, turns, functools.partial(second_k, rnd), ((), (zeros,) * 4)[rnd])
@@ -369,13 +375,17 @@
     reduce_start(1, reduce_wait(0))
     lax.fori_loop(turns - HELD, turns, functools.partial(second_k, rnd), ())
 
-    for rnd in range(ROUNDS):
-        for kind in range(2):
-            for side in range(2):
-                plane(rnd, kind, 0, side, lats).wait_send()
-                all_columns(rnd, kind, side).wait_send()
-    for k in range(1, n_day):
-        peer_copy(0, k).wait_send()
+    for kind in range(2):
+        pltpu.make_async_remote_copy(
+            src_ref=psend, dst_ref=precv, send_sem=plane_ss.at[kind], recv_sem=plane_rs.at[kind, 0, 0],
+            device_id=sides[0], device_id_type=MESH,
+        ).wait_send()
+    for side in range(2):
+        pltpu.make_async_remote_copy(
+            src_ref=csend, dst_ref=crecv.at[1 - side], send_sem=col_ss.at[side], recv_sem=col_rs.at[0, 0, 0],
+            device_id=beside[side], device_id_type=MESH,
+        ).wait_send()
+    all_peers(0).wait_send()
 
     all_sums = jnp.sum(reduce_wait(1), axis=1, keepdims=True)
     m1, n1, n2, n3, m2, zz, zu, uu = [jnp.broadcast_to(all_sums[i:i + 1], (1, lons)) for i in range(GROUP)]
@@ -389,8 +399,7 @@
     coefs[0:1] = a0 + a1 * (1.0 + beta)
     coefs[1:2] = a0 * a1
 
-    for k in range(1, n_lon):
-        peer_copy(1, k).wait_send()
+    all_peers(1).wait_send()
 
 
 def solution(mesh):
@@ -420,11 +429,11 @@
                 vmem(padded, f32), vmem(padded, f32), vmem(padded, f32),
                 vmem((ROUNDS, 2, lats, lons), f32), vmem((ROUNDS, 2, lats, lons), f32),
                 vmem((ROUNDS, 2, lats, lons), f32),
-                vmem((ROUNDS, 2, chunks, GROUP, lons), f32), vmem((ROUNDS, 2, 2, chunks, GROUP, lons), f32),
+                vmem((ROUNDS, 2, chunks, GROUP, lons), f32), vmem((2, ROUNDS, 2, chunks, GROUP, lons), f32),
                 vmem((2, GROUP, lons), f32), vmem((2, n_lon, GROUP, lons), f32),
-                dma((ROUNDS, 2, 2)), dma((ROUNDS, 2, chunks, 2)),
-                dma((ROUNDS, 2, 2)), dma((ROUNDS, 2, chunks, 2)),
-                dma((2, n_lon)), dma((2, n_lon)), dma((4,)),
+                dma((2,)), dma((2, chunks + chunks // TURN, 2)),
+                dma((2,)), dma((2, 2 * chunks // TURN, 2)),
+                dma((2,)), dma((2,)), dma((4,)),
             ],
             compiler_params=pltpu.CompilerParams(
                 collective_id=0, has_side_effects=True, vmem_limit_bytes=44 << 20

time: 52.6 us -> 51.8 us (0.985)
  Pallas kernels: 49.3 us -> 48.5 us
    pallas_call x1, Pallas kernels: 49.3 us -> 48.5 us  [per_device(): pl.pallas_call(functools.partial(kernel, names, n_day, n_lon), out_shape=...]
where the time goes in v6:
time: 51.8 us; the launch traced here: 51.7 us
  Pallas kernels  48.5 us (94%)
  other arithmetic  2.51 us (5%)
  between operations  0.65 us (1%)
    pallas_call x1, Pallas kernels, per_device(): pl.pallas_call(functools.partial(kernel, names, n_day, n_lon), out_shape=...  48.5 us
    add x1, other arithmetic, per_device(): residual = r0 - coefs[0] * q0 + coefs[1] * s  2.51 us

profile of v6, /device:TPU:1, one launch (start us, length us, event | category | flops | bytes accessed | tf_op | source)
XLA Modules:
  0.0 51.7 jit_solution(5886311663214786800)
XLA Ops:
  0.6 48.5 %shard_map.59 = (f32[4,1040,128]{2,1,0:T(8,128)S(1)}, f32[4,1040,128]{2,1,0:T(8,128)S(1)}, f32[4,1024,128]{2,1,0:T(8,128)S(1)}, f32[4,1024,128]{2,1,0:T(8,128)S(...) custom-call(f32[4,1024,128]{2,1,0:T(8,128)} %lat_h.1, f32[4,1024,128]{2,1,0:T(8,128)} %rs_h.1, ...), custom_call_target="tpu_custom_call" | custom-call | tf_op jit(solution)/shard_map/pallas_call | solution.py:418
  49.2 2.5 %multiply_add_fusion = (f32[4,1024,128]{2,1,0:T(8,128)}, f32[4,1024,128]{2,1,0:T(8,128)}) fusion(f32[4,1024,128]{2,1,0:T(8,128)S(1)} %get-tuple-element.13, f32[4,1024,128]{2,1,0:T(8,128)S(1)} %get-tuple-element.11, f32[4,1024,128]{2,1,0:T(8,128)S(1)} %get-tuple-element.12, f32[128]{0:T(128)S(1)} %get-tuple-element.17, f32[128]{0:T(128)S(1)} %get-tuple-element.16, ...), kind=kLoop, calls=%fused_computation | loop fusion | flops 3670016 | bytes 14681088 | tf_op jit(solution)/shard_map/add | solution.py:444
  (1 shorter events, 0.0 us)

commit v7 on v6

--- a/solution.py
+++ b/solution.py
@@ -402,6 +402,36 @@
     all_peers(1).wait_send()
 
 
+def finish(p0p, up, r0, q0, s, coefs, step_h, res_h, step, res, sems):
+    days, lats, lons = r0.shape
+    chunks = lats // CHUNK
+    coef_p = jnp.broadcast_to(coefs[0:1], (SMALL, lons))
+    coef_u = jnp.broadcast_to(coefs[1:2], (SMALL, lons))
+
+    def copies(c):
+        rows = pl.ds(c * CHUNK, CHUNK)
+        return (
+            pltpu.make_async_copy(step.at[:, rows], step_h.at[:, rows], sems.at[0, c]),
+            pltpu.make_async_copy(res.at[:, rows], res_h.at[:, rows], sems.at[1, c]),
+        )
+
+    def one(c, carry):
+        for b in range(CHUNK // SMALL):
+            row = pl.multiple_of(c * CHUNK + b * SMALL, SMALL)
+            rows, wide = pl.ds(row, SMALL), pl.ds(PAD + row, SMALL)
+            for d in range(days):
+                step[d, rows] = coef_p * p0p[d, wide] - coef_u * up[d, wide]
+                res[d, rows] = r0[d, rows] - coef_p * q0[d, rows] + coef_u * s[d, rows]
+        for copy in copies(c):
+            copy.start()
+        return carry
+
+    lax.fori_loop(0, chunks, one, 0)
+    for c in range(chunks):
+        for copy in copies(c):
+            copy.wait()
+
+
 def solution(mesh):
     names = tuple(mesh.axis_names)
     n_day, n_lon = mesh.shape["day"], mesh.shape["lon"]
@@ -439,9 +469,15 @@
                 collective_id=0, has_side_effects=True, vmem_limit_bytes=44 << 20
             ),
         )(latent, range_sq, counts, land)
-        body = slice(PAD, PAD + lats)
-        step = coefs[0] * p0[:, body] - coefs[1] * u[:, body]
-        residual = r0 - coefs[0] * q0 + coefs[1] * s
+        held = [pltpu.with_memory_space_constraint(v, pltpu.VMEM) for v in (p0, u, r0, q0, s, coefs)]
+        step, residual = pl.pallas_call(
+            finish,
+            out_shape=[jax.ShapeDtypeStruct(whole, f32)] * 2,
+            in_specs=[pl.BlockSpec(memory_space=pltpu.VMEM)] * 6,
+            out_specs=[pl.BlockSpec(memory_space=pl.ANY)] * 2,
+            scratch_shapes=[vmem(whole, f32), vmem(whole, f32), dma((2, chunks))],
+            compiler_params=pltpu.CompilerParams(vmem_limit_bytes=16 << 20),
+        )(*held)
         return step, residual
 
     return jax.shard_map(per_device, mesh=mesh, in_specs=(spec,) * 4, out_specs=(spec, spec), check_vma=False)

time: 51.8 us -> 51.5 us (level)
  other arithmetic: 2.51 us -> 0 us
  Pallas kernels: 48.5 us -> 50.7 us
    add x1 -> x0, other arithmetic: 2.51 us -> none  [per_device(): residual = r0 - coefs[0] * q0 + coefs[1] * s]
    pallas_call x0 -> x1, Pallas kernels: none -> 2.19 us  [per_device(): pl.pallas_call(finish, out_shape=[jax.ShapeDtypeStruct(whole, f32)] * 2,...]
where the time goes in v7:
time: 51.5 us; the launch traced here: 51.4 us
  Pallas kernels  50.7 us (98%)
  between operations  0.64 us (1%)
    pallas_call x1, Pallas kernels, per_device(): pl.pallas_call(functools.partial(kernel, names, n_day, n_lon), out_shape=...  48.5 us
    pallas_call x1, Pallas kernels, per_device(): pl.pallas_call(finish, out_shape=[jax.ShapeDtypeStruct(whole, f32)] * 2,...  2.19 us

profile of v7, /device:TPU:1, one launch (start us, length us, event | category | flops | bytes accessed | tf_op | source)
XLA Modules:
  0.0 51.4 jit_solution(12599399882959870168)
XLA Ops:
  0.6 48.5 %shard_map.59 = (f32[4,1040,128]{2,1,0:T(8,128)S(1)}, f32[4,1040,128]{2,1,0:T(8,128)S(1)}, f32[4,1024,128]{2,1,0:T(8,128)S(1)}, f32[4,1024,128]{2,1,0:T(8,128)S(...) custom-call(f32[4,1024,128]{2,1,0:T(8,128)} %lat_h.1, f32[4,1024,128]{2,1,0:T(8,128)} %rs_h.1, ...), custom_call_target="tpu_custom_call" | custom-call | tf_op jit(solution)/shard_map/pallas_call | solution.py:448
  49.2 2.2 %shard_map.60 = (f32[4,1024,128]{2,1,0:T(8,128)}, f32[4,1024,128]{2,1,0:T(8,128)}) custom-call(f32[4,1040,128]{2,1,0:T(8,128)S(1)} %get-tuple-element.8.p0p, f32[4,1040,128]{2,1,0:T(8,128)S(1)} %get-tuple-element.9.up, f32[4,1024,128]{2,1,0:T(8,128)S(1)} %get-tuple-element.10.r0, f32[4,1024,128]{2,1,0:T(8,128)S(1)} %get-tuple-element.11.q0, ...), custom_call_target="tpu_custom_call" | custom-call | tf_op jit(solution)/shard_map/pallas_call | solution.py:473
